TPU v7x, 128 devices: a whole 4x4x4 slice. The times are simulated.
128 devices in a mesh: row: 16 (over y_lo, z, core), col: 8 (over x, y_hi).
Axes of the slice: x: 4, y: 4 (y_hi: 2, y_lo: 2; y = y_hi * 2 + y_lo), z: 4, core: 2. Of those that a mesh axis runs over, the one named last changes fastest.
Arguments:
- tokens: bfloat16 [2048, 6144], P('row', 'col'), may hold values from -8 to 8
- cotangent: bfloat16 [2048, 6144], P('row', 'col'), may hold values from -6 to 6
- w_in: bfloat16 [6144, 12288], P('col', 'row'), may hold values from -0.078125 to 0.078125
- w_out: bfloat16 [12288, 6144], P('row', 'col'), may hold values from -0.18042196 to 0.18042196
- first_moment: float32 [6144, 12288], P('col', 'row'), may hold values from -0.6 to 0.6
- rotated_second_moment: float32 [6144, 12288], P('col', 'row'), may hold values from 0.01 to 0.05
- left_basis: float32 [6144, 768], P('col'), may hold values from -2 to 2
- right_basis: float32 [12288, 768], P('row'), may hold values from -2 to 2
Outputs:
- layer_out: bfloat16 [2048, 6144], P('row', 'col')
- input_grad: bfloat16 [2048, 6144], P('row', 'col')
- out_grad: bfloat16 [12288, 6144], P('row', 'col')
- update: float32 [6144, 12288], P('col', 'row')
- new_first: float32 [6144, 12288], P('col', 'row')
- new_second: float32 [6144, 12288], P('col', 'row')
- left_stat: float32 [6144, 768], P(('col', 'row'))
- right_stat: float32 [12288, 768], P(('row', 'col'))
All inputs are finite; a program needn't handle non-finite values.
Results may differ from a plain program's by a relative error of at most 0.022.
Values may be sent and summed in bfloat16 or wider, within the bound.
No kernel may reach another device: no remote copies, remote signals or barrier semaphores. Data moves between devices by JAX's collectives and lax.ppermute only.
A program may use at most 128 MiB of HBM per device.

v0:
```python
import jax
import jax.numpy as jnp
from jax import lax
from jax.experimental import pallas as pl
from jax.experimental.pallas import tpu as pltpu
from jax.sharding import Mesh, PartitionSpec as P

D = 6144
HID = 12288

bf16 = jnp.bfloat16
f32 = jnp.float32

ROW = ("yl", "z", "c")
COL = ("x", "yh")
SIZES = {"yl": 2, "z": 4, "c": 2, "x": 4, "yh": 2}


def gelu_pair(hidden):
    normal_cdf = 0.5 * (1.0 + jax.scipy.special.erf(hidden * 0.7071067811865476))
    activation = hidden * normal_cdf
    derivative = normal_cdf + hidden * jnp.exp(-0.5 * hidden * hidden) * 0.3989422804014327
    return (activation, derivative)


def shift(value, axis, by):
    size = SIZES[axis]
    return lax.ppermute(value, axis, [(i, (i + by) % size) for i in range(size)])


def add(*terms):
    total = terms[0].astype(f32)
    for term in terms[1:]:
        total = total + term.astype(f32)
    return total


def matmul(a, b, ca=1, cb=0):
    return lax.dot_general(a, b, (((ca,), (cb,)), ((), ())), preferred_element_type=f32)


def ring_send(parts, ring):
    return [shift(parts[k].astype(bf16), ring, k) for k in (2, 1, 3)]


def ring_gather(block):
    return [shift(block, "x", -k) for k in (1, 2, 3)]


def whole(shape):
    return pl.BlockSpec(shape, lambda *_: (0,) * len(shape))


def call(kernel, scalars, grid, in_specs, out_specs, out_shape, scratch, flops, *args):
    moved = sum(v.size * v.dtype.itemsize for v in args) + sum(
        v.size * jnp.dtype(v.dtype).itemsize for v in jax.tree.leaves(out_shape)
    )
    return pl.pallas_call(
        kernel,
        out_shape=out_shape,
        grid_spec=pltpu.PrefetchScalarGridSpec(
            num_scalar_prefetch=1,
            grid=grid,
            in_specs=in_specs,
            out_specs=out_specs,
            scratch_shapes=scratch,
        ),
        compiler_params=pltpu.CompilerParams(vmem_limit_bytes=50 * 2**20),
        cost_estimate=pl.CostEstimate(flops=flops, bytes_accessed=moved, transcendentals=0),
    )(jnp.stack([jnp.asarray(v, jnp.int32) for v in scalars]), *args)


def gram_terms(weight_grad, z, c, x, yh):
    size = weight_grad.shape[0]
    left_rows, right_rows = size // 16, size // 8

    def kernel(at, weight_ref, *refs):
        send_ref, keep_ref = refs[:2]
        right_refs, (left, right) = refs[2:6], refs[6:]
        weight = weight_ref[...]
        here, turned = weight.astype(bf16), weight.T.astype(bf16)
        left[...] = (matmul(here, turned) * (1.0 / HID)).reshape(16, left_rows, size)
        right[...] = (matmul(turned, here) * (1.0 / D)).reshape(8, right_rows, size)
        for k in range(4):
            along_z, along_x = lax.rem(at[0] + k, 4), lax.rem(at[2] + k, 4)
            for y in range(2):
                row = y * 8 + along_z * 2
                send_ref[k, y] = left[row + 1 - at[1]].astype(bf16)
                keep_ref[k, y] = left[row + at[1]].astype(bf16)
                other = at[3] if y == 0 else 1 - at[3]
                right_refs[k][y] = right[along_x * 2 + other].astype(bf16)

    shapes = [(4, 2, left_rows, size)] * 2 + [(2, right_rows, size)] * 4
    return call(
        kernel,
        [z, c, x, yh],
        (1,),
        [whole((size, size))],
        [whole(v) for v in shapes],
        [jax.ShapeDtypeStruct(v, bf16) for v in shapes],
        [
            pltpu.VMEM((16, left_rows, size), f32),
            pltpu.VMEM((8, right_rows, size), f32),
        ],
        4 * size**3,
        weight_grad,
    )


def core_sums(z, c, tokens, left):
    width = left[0].shape[-1]
    left = [v.reshape(4, -1, width) for v in left]
    rows = tokens[0][1].shape[2] if tokens else 0
    shape = (2 * len(tokens) * rows + left[0].shape[1], width)
    args = [v for pair in tokens for v in pair] + left

    def kernel(at, *refs):
        ins, outs = refs[: len(args)], refs[len(args) :]
        for k in range(4):
            place = lax.rem(at[0] + k, 4)
            start = 0
            for i in range(len(tokens)):
                for y in range(2):
                    total = ins[2 * i][y, place, at[1]].astype(f32) + ins[2 * i + 1][y, place].astype(f32)
                    outs[k][start : start + rows] = total.astype(outs[k].dtype)
                    start += rows
            total = ins[-2][k].astype(f32) + ins[-1][k].astype(f32)
            outs[k][start:] = total.astype(outs[k].dtype)

    return call(
        kernel,
        [z, c],
        (1,),
        [whole(v.shape) for v in args],
        [whole(shape)] * 4,
        [jax.ShapeDtypeStruct(shape, bf16 if k else f32) for k in range(4)],
        [],
        0,
        *args,
    )


def split(value):
    high = value.astype(bf16)
    return high, (value - high.astype(f32)).astype(bf16)


def basis_parts(left_basis, right_basis):
    def kernel(_, left_ref, right_ref, rounded_ref, left_high, left_low, right_high, right_low):
        rounded_ref[...] = left_ref[...].astype(bf16)
        left_high[...], left_low[...] = split(left_ref[...].T)
        right_high[...], right_low[...] = split(right_ref[...])

    shape = left_basis.shape
    out = jax.ShapeDtypeStruct(shape, bf16)
    return call(kernel, [0], (1,), [whole(shape)] * 2, [whole(shape)] * 5, [out] * 5, [], 0, left_basis, right_basis)


def rotated_step(weight_grad, bases, first_moment, second_moment):
    size = weight_grad.shape[0]
    parts = 3 if size % 384 == 0 else 1
    cut = size // parts

    def fine(a, b):
        return matmul(a[0], b[0]) + (matmul(a[0], b[1]) + matmul(a[1], b[0]))

    def kernel(_, w_ref, l_ref, th_ref, tl_ref, rh_ref, rl_ref, m_ref, v_ref, *refs):
        first_ref, second_ref, update_ref, high, low = refs
        step = pl.program_id(0)

        @pl.when(step == 0)
        def _():
            turned = fine((th_ref[...], tl_ref[...]), split(w_ref[...]))
            high[...], low[...] = split(turned)

        right = rh_ref[...], rl_ref[...]
        rotated = fine((high[...], low[...]), right)
        new_first = 0.9 * m_ref[...] + 0.1 * rotated
        new_second = 0.95 * v_ref[...] + 0.05 * rotated * rotated
        first_ref[...] = new_first
        second_ref[...] = new_second
        ratio = new_first / (jnp.sqrt(new_second) + 1e-08)
        back = matmul(l_ref[...], ratio.astype(bf16))
        update = matmul(back.astype(bf16), right[0], 1, 1)

        @pl.when(step == 0)
        def _():
            update_ref[...] = update

        @pl.when(step > 0)
        def _():
            update_ref[...] += update

    columns = pl.BlockSpec((size, cut), lambda i, _: (0, i))
    out = jax.ShapeDtypeStruct((size, size), f32)
    return call(
        kernel,
        [0],
        (parts,),
        [whole((size, size))] * 4 + [columns] * 4,
        [columns, columns, whole((size, size))],
        [out] * 3,
        [pltpu.VMEM((size, size), bf16)] * 2,
        16 * size**3,
        weight_grad,
        *bases,
        first_moment,
        second_moment,
    )


def shards(
    tokens, cotangent, w_in, w_out, first_moment, rotated_second_moment, left_basis, right_basis
):
    yl, z, c, x, yh = (lax.axis_index(name) for name in ROW + COL)
    rows, width = tokens.shape
    token_count = 16 * rows
    half, block = token_count // 2, token_count // 8
    grad_scale = token_count ** (-0.5)

    def bf(value):
        return value.astype(bf16)

    def halves(value):
        parts = value.reshape(2, rows // 2, width)
        return [lax.dynamic_index_in_dim(parts, at, 0, False) for at in (yh, 1 - yh)]

    both = lax.all_gather(jnp.stack(halves(tokens) + halves(cotangent)), ROW, axis=1, tiled=True)
    w_in_turned, w_out_turned, bases = lax.optimization_barrier(
        (w_in.T, w_out.T, basis_parts(left_basis, right_basis))
    )

    leaving = bf(matmul(both[3], w_out_turned))
    back_arrived = shift(leaving, "yh", 1)
    leaving, w_in_later = lax.optimization_barrier((leaving, w_in))
    terms = bf(matmul(both[:2].reshape(token_count, width), w_in_later)).reshape(2, half, width)
    forward = lax.psum_scatter(terms, "x", scatter_dimension=1, tiled=True)
    staying = matmul(both[2], w_out_turned)
    line = both[:2].reshape(token_count, width).T
    back_arrived, staying, line = lax.optimization_barrier((back_arrived, staying, line))

    total = bf(add(staying, back_arrived))
    parts = [lax.dynamic_slice_in_dim(total, ((x + k) % 4) * block, block, 0) for k in range(4)]
    back = ring_send(parts, "x")
    parts, forward = lax.optimization_barrier((parts, forward))
    activation, derivative = gelu_pair(add(forward[0], shift(forward[1], "yh", 1)))
    act, derivative, back = lax.optimization_barrier((bf(activation), derivative, back))

    acts = ring_gather(act)
    grad = bf(add(parts[0], *back) * derivative)
    pair = shift(grad, "yh", 1)
    acts, grad, pair = lax.optimization_barrier((acts, grad, pair))

    grads = lax.all_gather(jnp.stack([grad, pair]), "x", axis=1, tiled=True)
    turned = jnp.concatenate([act] + acts + [act] + acts[:2])
    act_own = lax.dynamic_slice_in_dim(turned, ((4 - x) % 4) * block, half, 0)
    act_other = shift(act_own, "yh", 1)
    mixed_own = bf(matmul(act_own, w_out))
    out_grad = matmul(act_own, both[2], 0, 0)
    act_other, mixed_own, out_grad = lax.optimization_barrier((act_other, mixed_own, out_grad))
    mixed = jnp.concatenate([mixed_own, bf(matmul(act_other, w_out))])
    grads, mixed = lax.optimization_barrier((grads, mixed))

    carried = bf(matmul(grads.reshape(token_count, width), w_in_turned))
    terms = jnp.concatenate([mixed, carried]).reshape(8, half // 2, width)
    sums = lax.psum_scatter(terms, ("z", "c"), scatter_dimension=1, tiled=True)
    terms, grads = lax.optimization_barrier((terms, grads))
    weight_grad = grad_scale * (matmul(line[:, :half], grads[0]) + matmul(line[:, half:], grads[1]))
    left_send, left_keep, *right = gram_terms(weight_grad, z, c, x, yh)
    left_arrived = shift(left_send, "c", 1)
    left_arrived, right, weight_grad = lax.optimization_barrier((left_arrived, right, weight_grad))
    chip = core_sums(z, c, [], (left_keep, left_arrived))
    chip_arrived = ring_send(chip, "z")
    right_arrived = ring_send(right, "x")
    new_first, new_second, update = rotated_step(weight_grad, bases, first_moment, rotated_second_moment)
    chip, chip_arrived, right_arrived, update, act_other = lax.optimization_barrier(
        (chip, chip_arrived, right_arrived, update, act_other)
    )

    right_own = add(*[v[0] for v in (right[0], *right_arrived)])
    right_other = bf(add(*[v[1] for v in (right[0], *right_arrived)]))
    right_stat = add(right_own, shift(right_other, "yh", 1))
    out_grad = bf(grad_scale * (out_grad + matmul(act_other, both[3], 0, 0)))
    left = add(chip[0], *chip_arrived).reshape(2, -1, width)

    def along_yl(value, axis):
        mine, theirs = (lax.dynamic_index_in_dim(value, at, axis, False) for at in (yl, 1 - yl))
        return mine.reshape(-1, width), bf(theirs.reshape(-1, width))

    left_mine, left_theirs = along_yl(left, 0)
    left_stat = add(left_mine, shift(left_theirs, "yl", 1))
    mine, theirs = along_yl(sums.reshape(4, 2, rows // 2, width), 1)
    last = bf(add(mine, shift(theirs, "yl", 1)))
    mixed, carried = last[:rows], last[rows:]

    def ordered(value):
        own, other = value[: rows // 2], value[rows // 2 :]
        return jnp.concatenate([jnp.where(yh == 0, own, other), jnp.where(yh == 0, other, own)])

    layer_out, input_grad = ordered(mixed), ordered(carried)
    return (layer_out, input_grad, out_grad, update, new_first, new_second, left_stat, right_stat)


def solution(mesh):
    fine = Mesh(mesh.devices.reshape(2, 4, 2, 4, 2), ROW + COL)
    in_specs = (
        P(ROW, COL),
        P(ROW, COL),
        P(COL, ROW),
        P(ROW, COL),
        P(COL, ROW),
        P(COL, ROW),
        P(COL, None),
        P(ROW, None),
    )
    out_specs = (
        P(ROW, COL),
        P(ROW, COL),
        P(ROW, COL),
        P(COL, ROW),
        P(COL, ROW),
        P(COL, ROW),
        P(COL + ROW, None),
        P(ROW + COL, None),
    )
    return jax.shard_map(shards, mesh=fine, in_specs=in_specs, out_specs=out_specs, check_vma=False)
```

profile of v0, /device:TPU:2, one launch (start us, length us, event | category | flops | bytes accessed | tf_op | source)
XLA Modules:
  0.0 280.9 jit_solution(8357825756826687765)
XLA Ops:
  9.3 4.8 %shard_map.143 = (bf16[768,768]{1,0:T(8,128)(2,1)S(1)}, bf16[768,768]{1,0:T(8,128)(2,1)S(1)}, bf16[768,768]{1,0:T(8,128)(2,1)S(1)}, bf16[768,768]{1,0:T(8,128)(2,1)}, bf16[768,768]{1,0:T(8,128)(2,1)}) custom-call(s32[1]{0:T(128)} %constant.84.clone.1._, f32[768,768]{1,0:T(8,128)} %left_ref.1, f32[768,768]{1,0:T(8,128)} %right_ref.1), custom_call_target="tpu_custom_call" | custom-call | bytes 10616832 | tf_op jit(solution)/shard_map/pallas_call | solution.py:58
  16.1 39.0 %all-gather.3.cloned.1.call-done = bf16[4,1024,768]{2,1,0:T(8,128)(2,1)} async-done(((bf16[4,64,768]{2,1,0:T(8,128)(2,1)}), bf16[4,1024,768]{2,1,0:T(8,128)(2,1)}) %all-gather.3.cloned.1.call-update) | async-done | bytes 6291472 | tf_op jit(solution)/shard_map/all_gather | solution.py:228
  55.1 4.1 %convolution_convert_fusion.4 = bf16[1024,768]{1,0:T(8,128)(2,1)} fusion(bf16[768,768]{0,1:T(8,128)(2,1)S(1)} %bitcast.76, bf16[4,1024,768]{2,1,0:T(8,128)(2,1)} %all-gather.3.cloned.1.call-done), kind=kOutput, calls=%fused_computation.9 | convolution fusion | flops 1208745984 | bytes 4325376 | tf_op jit(solution)/shard_map/dot_general | solution.py:39
  59.4 1.4 copy-done.17
  60.8 4.0 %convolution_convert_fusion.1 = bf16[2048,768]{1,0:T(8,128)(2,1)} fusion(bf16[2048,768]{1,0:T(8,128)(2,1)S(1)} %bitcast.80, bf16[768,768]{1,0:T(8,128)(2,1)S(1)} %copy-done.17), kind=kOutput, calls=%fused_computation.2 | convolution fusion | flops 2417491968 | bytes 7471104 | tf_op jit(solution)/shard_map/dot_general | solution.py:39
  64.9 2.9 %collective-permute-start = (bf16[1024,768]{1,0:T(8,128)(2,1)}, bf16[1024,768]{1,0:T(8,128)(2,1)}, u32[]{:S(2)}, u32[]{:S(2)}) collective-permute-start(bf16[1024,768]{1,0:T(8,128)(2,1)} %convolution_convert_fusion.4), channel_id=1, source_target_pairs={{0,1},{1,0},{2,3},{3,2},{4,5},{5,4},{6,7},{7,6},{8,9},{9,8},{10,11... | collective-permute-start | bytes 4718600 | tf_op jit(solution)/shard_map/ppermute | solution.py:28
  67.8 2.8 %fusion.14 = f32[1024,768]{1,0:T(8,128)S(1)} fusion(bf16[768,768]{0,1:T(8,128)(2,1)S(1)} %bitcast.75, bf16[4,1024,768]{2,1,0:T(8,128)(2,1)} %all-gather.3.cloned.1.call-done), kind=kOutput, calls=%fused_computation.22 | convolution fusion | flops 1207959552 | bytes 5898240 | tf_op jit(solution)/shard_map/dot_general | solution.py:39
  70.7 32.7 %collective-permute-done = bf16[1024,768]{1,0:T(8,128)(2,1)} collective-permute-done((bf16[1024,768]{1,0:T(8,128)(2,1)}, bf16[1024,768]{1,0:T(8,128)(2,1)}, u32[]{:S(2)}, u32[]{:S(2)}) %collective-permute-start) | collective-permute-done | bytes 1572896 | tf_op jit(solution)/shard_map/ppermute | solution.py:28
  103.3 1.9 add_convert_fusion
  107.2 2.9 %collective-permute-start.1 = (bf16[256,768]{1,0:T(8,128)(2,1)S(1)}, bf16[256,768]{1,0:T(8,128)(2,1)S(1)}, u32[]{:S(2)}, u32[]{:S(2)}) collective-permute-start(bf16[256,768]{1,0:T(8,128)(2,1)S(1)} %slice_bitcast_fusion.6), channel_id=1, source_target_pairs={{0,1},{1,0},{2,3},{3,2},{4,5},{5,4},{6,7},{7,6},{8,9},{9,8},{10,11... | collective-permute-start | bytes 1179656 | tf_op jit(solution)/shard_map/ppermute | solution.py:28
  110.2 2.1 collective-permute-start.2
  112.3 2.0 collective-permute-start.4
  114.3 5.0 %collective-permute-done.1 = bf16[256,768]{1,0:T(8,128)(2,1)S(1)} collective-permute-done((bf16[256,768]{1,0:T(8,128)(2,1)S(1)}, bf16[256,768]{1,0:T(8,128)(2,1)S(1)}, u32[]{:S(2)}, u32[]{:S(2)}) %collective-permute-start.1) | collective-permute-done | bytes 393248 | tf_op jit(solution)/shard_map/ppermute | solution.py:28
  119.3 1.4 fusion.18
  120.7 3.3 %collective-permute-done.2 = bf16[256,768]{1,0:T(8,128)(2,1)S(1)} collective-permute-done((bf16[256,768]{1,0:T(8,128)(2,1)}, bf16[256,768]{1,0:T(8,128)(2,1)S(1)}, u32[]{:S(2)}, u32[]{:S(2)}) %collective-permute-start.2) | collective-permute-done | bytes 393248 | tf_op jit(solution)/shard_map/ppermute | solution.py:28
  124.0 6.6 %collective-permute-done.3 = bf16[256,768]{1,0:T(8,128)(2,1)S(1)} collective-permute-done((bf16[256,768]{1,0:T(8,128)(2,1)}, bf16[256,768]{1,0:T(8,128)(2,1)S(1)}, u32[]{:S(2)}, u32[]{:S(2)}) %collective-permute-start.3) | collective-permute-done | bytes 393248 | tf_op jit(solution)/shard_map/ppermute | solution.py:28
  132.1 1.5 collective-permute-start.6
  133.5 2.6 collective-permute-start.7
  136.2 7.2 %collective-permute-done.8 = bf16[256,768]{1,0:T(8,128)(2,1)S(1)} collective-permute-done((bf16[256,768]{1,0:T(8,128)(2,1)S(1)}, bf16[256,768]{1,0:T(8,128)(2,1)S(1)}, u32[]{:S(2)}, u32[]{:S(2)}) %collective-permute-start.8) | collective-permute-done | bytes 393248 | tf_op jit(solution)/shard_map/ppermute | solution.py:28
  143.3 7.6 %collective-permute-done.6 = bf16[256,768]{1,0:T(8,128)(2,1)S(1)} collective-permute-done((bf16[256,768]{1,0:T(8,128)(2,1)S(1)}, bf16[256,768]{1,0:T(8,128)(2,1)S(1)}, u32[]{:S(2)}, u32[]{:S(2)}) %collective-permute-start.6) | collective-permute-done | bytes 393248 | tf_op jit(solution)/shard_map/ppermute | solution.py:28
  151.0 1.5 collective-permute-done.7
  155.5 3.1 %collective-permute-start.9 = (bf16[1024,768]{1,0:T(8,128)(2,1)S(1)}, bf16[1024,768]{1,0:T(8,128)(2,1)S(1)}, u32[]{:S(2)}, u32[]{:S(2)}) collective-permute-start(bf16[1024,768]{1,0:T(8,128)(2,1)S(1)} %constant_dynamic-slice_fusion.2), channel_id=1, source_target_pairs={{0,1},{1,0},{2,3},{3,2},{4,5},{5,4},{6,7},{7,6},{8,9},{9,8},{10,11... | collective-permute-start | bytes 4718600 | tf_op jit(solution)/shard_map/ppermute | solution.py:28
  158.7 1.4 convolution_convert_fusion.3
  160.1 4.3 %fusion.13 = f32[768,768]{1,0:T(8,128)} fusion(bf16[1024,768]{1,0:T(8,128)(2,1)S(1)} %constant_dynamic-slice_fusion.2, bf16[4,1024,768]{2,1,0:T(8,128)(2,1)} %all-gather.3.cloned.1.call-done), kind=kOutput, calls=%fused_computation.21 | convolution fusion | flops 1207959552 | bytes 5505024 | tf_op jit(solution)/shard_map/dot_general | solution.py:39
  164.4 28.2 %collective-permute-done.9 = bf16[1024,768]{1,0:T(8,128)(2,1)S(1)} collective-permute-done((bf16[1024,768]{1,0:T(8,128)(2,1)S(1)}, bf16[1024,768]{1,0:T(8,128)(2,1)S(1)}, u32[]{:S(2)}, u32[]{:S(2)}) %collective-permute-start.9) | collective-permute-done | bytes 1572896 | tf_op jit(solution)/shard_map/ppermute | solution.py:28
  193.8 1.4 convolution_convert_fusion.2
  195.2 1.9 pad_maximum_fusion.1
  197.1 4.7 %convolution_convert_fusion = bf16[2048,768]{1,0:T(8,128)(2,1)S(1)} fusion(bf16[2048,768]{1,0:T(8,128)(2,1)} %bitcast.92, bf16[768,768]{0,1:T(8,128)(2,1)S(1)} %bitcast.93), kind=kOutput, calls=%fused_computation.1 | convolution fusion | flops 2417491968 | bytes 7471104 | tf_op jit(solution)/shard_map/dot_general | solution.py:39
  201.8 3.1 %pad_maximum_fusion = bf16[4096,768]{1,0:T(8,128)(2,1)} fusion(bf16[2048,768]{1,0:T(8,128)(2,1)S(1)} %convolution_convert_fusion, bf16[2048,768]{1,0:T(8,128)(2,1)S(1)} %copy-done.6), kind=kLoop, calls=%fused_computation | loop fusion | flops 12582912 | bytes 12582912 | tf_op jit(solution)/shard_map/concatenate | solution.py:265
  205.0 3.5 %fusion = f32[768,768]{1,0:T(8,128)S(1)} fusion(bf16[2,1024,768]{2,1,0:T(8,128)(2,1)} %all-gather.5.cloned.1.call-done, bf16[768,2048]{0,1:T(8,128)(2,1)} %bitcast.81), kind=kOutput, calls=%fused_computation.12 | convolution fusion | flops 1207959552 | bytes 5505024 | tf_op jit(solution)/shard_map/dot_general | solution.py:39
  208.8 2.9 %add_multiply_fusion.weight_ref.w_ref = f32[768,768]{1,0:T(8,128)} fusion(f32[768,768]{1,0:T(8,128)S(1)} %fusion, bf16[2,1024,768]{2,1,0:T(8,128)(2,1)S(1)} %copy-done.14, bf16[768,2048]{0,1:T(8,128)(2,1)S(1)} %bitcast.82), kind=kOutput, calls=%fused_computation.6 | convolution fusion | flops 1209139200 | bytes 7864320 | tf_op jit(solution)/shard_map/dot_general | solution.py:39
  211.7 4.5 %shard_map.144 = (bf16[4,2,48,768]{3,2,1,0:T(8,128)(2,1)S(1)}, bf16[4,2,48,768]{3,2,1,0:T(8,128)(2,1)S(1)}, bf16[2,96,768]{2,1,0:T(8,128)(2,1)S(1)}, bf16[2,96,7...) custom-call(s32[4]{0:T(128)S(1)} %pad_add_fusion.1.at, ...), custom_call_target="tpu_custom_call" | custom-call | flops 1811939328 | bytes 4718592 | tf_op jit(solution)/shard_map/pallas_call | solution.py:58
  216.4 1.9 collective-permute-done.11
  218.9 2.8 collective-permute-start.12
  222.6 2.4 collective-permute-start.14
  225.0 2.1 collective-permute-start.15
  227.1 3.5 %collective-permute-start.16 = (bf16[2,96,768]{2,1,0:T(8,128)(2,1)S(1)}, bf16[2,96,768]{2,1,0:T(8,128)(2,1)S(1)}, u32[]{:S(2)}, u32[]{:S(2)}) collective-permute-start(bf16[2,96,768]{2,1,0:T(8,128)(2,1)S(1)} %get-tuple-element.111), channel_id=1, source_target_pairs={{0,2},{2,4},{4,6},{6,0},{1,3},{3,5},{5,7},{7,1},{8,10},{10,12},{12... | collective-permute-start | bytes 884744 | tf_op jit(solution)/shard_map/ppermute | solution.py:28
  230.6 2.2 collective-permute-start.17
  232.8 1.3 copy-done.3
  234.1 1.3 copy-done.5
  235.4 17.6 %shard_map.146 = (f32[768,768]{1,0:T(8,128)}, f32[768,768]{1,0:T(8,128)}, f32[768,768]{1,0:T(8,128)}) custom-call(s32[1]{0:T(128)} %constant.84.clone.1._, f32[768,768]{1,0:T(8,128)} %add_multiply_fusion.weight_ref.w_ref, bf16[768,768]{1,0:T(8,128)(2,1)S(1)} %get-tuple-element.114.l_ref, bf16[768,768]{1,0:T(8,128)(2,1)S(1)} %copy-done.3, ...), custom_call_target="tpu_custom_call" | custom-call | flops 7247757312 | bytes 20054016 | tf_op jit(solution)/shard_map/pallas_call | solution.py:58
  253.1 3.0 %collective-permute-start.19 = (bf16[96,768]{1,0:T(8,128)(2,1)S(1)}, bf16[96,768]{1,0:T(8,128)(2,1)S(1)}, u32[]{:S(2)}, u32[]{:S(2)}) collective-permute-start(bf16[96,768]{1,0:T(8,128)(2,1)S(1)} %fusion.20), channel_id=1, source_target_pairs={{0,1},{1,0},{2,3},{3,2},{4,5},{5,4},{6,7},{7,6},{8,9},{9,8},{10,11... | collective-permute-start | bytes 442376 | tf_op jit(solution)/shard_map/ppermute | solution.py:28
  257.8 3.0 %fusion.12 = f32[768,768]{1,0:T(8,128)S(1)} fusion(bf16[1024,768]{1,0:T(8,128)(2,1)S(1)} %copy-done.16, bf16[4,1024,768]{2,1,0:T(8,128)(2,1)} %all-gather.3.cloned.1.call-done), kind=kOutput, calls=%fused_computation.20 | convolution fusion | flops 1207959552 | bytes 5505024 | tf_op jit(solution)/shard_map/dot_general | solution.py:39
  260.8 1.4 multiply_convert_fusion
  263.4 1.5 collective-permute-start.10
  264.9 1.6 bitcast_add_fusion.1
  266.5 1.7 bitcast_add_fusion
  268.2 4.6 %collective-permute-done.10 = bf16[256,768]{1,0:T(8,128)(2,1)S(1)} collective-permute-done((bf16[256,768]{1,0:T(8,128)(2,1)S(1)}, bf16[256,768]{1,0:T(8,128)(2,1)S(1)}, u32[]{:S(2)}, u32[]{:S(2)}) %collective-permute-start.10) | collective-permute-done | bytes 393248 | tf_op jit(solution)/shard_map/ppermute | solution.py:28
  (88 shorter events, 18.7 us)
Async XLA Ops:
  7.2 8.9 %copy-start = (bf16[768,768]{1,0:T(8,128)(2,1)S(1)}, bf16[768,768]{1,0:T(8,128)(2,1)}, u32[]{:S(2)}) copy-start(bf16[768,768]{1,0:T(8,128)(2,1)} %param.11) | copy-start | bytes 3538948
  7.2 47.9 %all-gather.3.cloned.1.call-start = ((), (), s32[]{:S(2)}) async-start(), calls=%async_computation.2 | async-start | bytes 6684672 | tf_op jit(solution)/shard_map/all_gather | solution.py:228
  9.2 97.0 %reduce-scatter.3.cloned.1.call-start = ((), (), s32[]{:S(2)}) async-start(), calls=%async_computation.3 | async-start | bytes 3932160 | tf_op jit(solution)/shard_map/reduce_scatter | solution.py:237
  14.0 1.0 copy-start.2
  15.1 1.0 copy-start.4
  55.1 4.1 %copy-start.10 = (bf16[4,1024,768]{2,1,0:T(8,128)(2,1)S(1)}, bf16[4,1024,768]{2,1,0:T(8,128)(2,1)}, u32[]{:S(2)}) copy-start(bf16[4,1024,768]{2,1,0:T(8,128)(2,1)} %all-gather.3.cloned.1.call-done) | copy-start | bytes 18874372
  59.2 1.6 copy-start.17
  59.4 5.4 %copy-start.7 = (bf16[2,1024,768]{2,1,0:T(8,128)(2,1)}, bf16[2,1024,768]{2,1,0:T(8,128)(2,1)S(1)}, u32[]{:S(2)}) copy-start(bf16[2,1024,768]{2,1,0:T(8,128)(2,1)S(1)} %slice.95) | copy-start | bytes 9437188
  64.8 132.2 %all-gather.5.cloned.1.call-start = ((), (), s32[]{:S(2)}) async-start(), calls=%async_computation.4 | async-start | bytes 3932160 | tf_op jit(solution)/shard_map/all_gather | solution.py:254
  64.9 38.4 %collective-permute-start = (bf16[1024,768]{1,0:T(8,128)(2,1)}, bf16[1024,768]{1,0:T(8,128)(2,1)}, u32[]{:S(2)}, u32[]{:S(2)}) collective-permute-start(bf16[1024,768]{1,0:T(8,128)(2,1)} %convolution_convert_fusion.4), channel_id=1, source_target_pairs={{0,1},{1,0},{2,3},{3,2},{4,5},{5,4},{6,7},{7,6},{8,9},{9,8},{10,11... | collective-permute-start | bytes 4718600 | tf_op jit(solution)/shard_map/ppermute | solution.py:28
  107.2 12.0 %collective-permute-start.1 = (bf16[256,768]{1,0:T(8,128)(2,1)S(1)}, bf16[256,768]{1,0:T(8,128)(2,1)S(1)}, u32[]{:S(2)}, u32[]{:S(2)}) collective-permute-start(bf16[256,768]{1,0:T(8,128)(2,1)S(1)} %slice_bitcast_fusion.6), channel_id=1, source_target_pairs={{0,1},{1,0},{2,3},{3,2},{4,5},{5,4},{6,7},{7,6},{8,9},{9,8},{10,11... | collective-permute-start | bytes 1179656 | tf_op jit(solution)/shard_map/ppermute | solution.py:28
  110.2 13.8 %collective-permute-start.2 = (bf16[256,768]{1,0:T(8,128)(2,1)}, bf16[256,768]{1,0:T(8,128)(2,1)S(1)}, u32[]{:S(2)}, u32[]{:S(2)}) collective-permute-start(bf16[256,768]{1,0:T(8,128)(2,1)} %get-tuple-element.133), channel_id=1, source_target_pairs={{0,4},{2,6},{4,0},{6,2},{1,5},{3,7},{5,1},{7,3},{8,12},{10,14},{12... | collective-permute-start | bytes 1179656 | tf_op jit(solution)/shard_map/ppermute | solution.py:28
  112.3 18.3 %collective-permute-start.3 = (bf16[256,768]{1,0:T(8,128)(2,1)}, bf16[256,768]{1,0:T(8,128)(2,1)S(1)}, u32[]{:S(2)}, u32[]{:S(2)}) collective-permute-start(bf16[256,768]{1,0:T(8,128)(2,1)} %get-tuple-element.134), channel_id=1, source_target_pairs={{0,2},{2,4},{4,6},{6,0},{1,3},{3,5},{5,7},{7,1},{8,10},{10,12},{12... | collective-permute-start | bytes 1179656 | tf_op jit(solution)/shard_map/ppermute | solution.py:28
  112.3 18.3 %collective-permute-start.4 = (bf16[256,768]{1,0:T(8,128)(2,1)S(1)}, bf16[256,768]{1,0:T(8,128)(2,1)S(1)}, u32[]{:S(2)}, u32[]{:S(2)}) collective-permute-start(bf16[256,768]{1,0:T(8,128)(2,1)S(1)} %get-tuple-element.132), channel_id=1, source_target_pairs={{0,6},{2,0},{4,2},{6,4},{1,7},{3,1},{5,3},{7,5},{8,14},{10,8},{12,... | collective-permute-start | bytes 1179656 | tf_op jit(solution)/shard_map/ppermute | solution.py:28
  130.8 12.6 %collective-permute-start.8 = (bf16[256,768]{1,0:T(8,128)(2,1)S(1)}, bf16[256,768]{1,0:T(8,128)(2,1)S(1)}, u32[]{:S(2)}, u32[]{:S(2)}) collective-permute-start(bf16[256,768]{1,0:T(8,128)(2,1)S(1)} %multiply_convert_fusion.1), channel_id=1, source_target_pairs={{0,1},{1,0},{2,3},{3,2},{4,5},{5,4},{6,7},{7,6},{8,9},{9,8},{10,11... | collective-permute-start | bytes 1179656 | tf_op jit(solution)/shard_map/ppermute | solution.py:28
  131.5 11.8 %collective-permute-start.5 = (bf16[256,768]{1,0:T(8,128)(2,1)S(1)}, bf16[256,768]{1,0:T(8,128)(2,1)S(1)}, u32[]{:S(2)}, u32[]{:S(2)}) collective-permute-start(bf16[256,768]{1,0:T(8,128)(2,1)S(1)} %get-tuple-element.80), channel_id=1, source_target_pairs={{0,6},{2,0},{4,2},{6,4},{1,7},{3,1},{5,3},{7,5},{8,14},{10,8},{12,... | collective-permute-start | bytes 1179656 | tf_op jit(solution)/shard_map/ppermute | solution.py:28
  132.1 18.9 %collective-permute-start.6 = (bf16[256,768]{1,0:T(8,128)(2,1)S(1)}, bf16[256,768]{1,0:T(8,128)(2,1)S(1)}, u32[]{:S(2)}, u32[]{:S(2)}) collective-permute-start(bf16[256,768]{1,0:T(8,128)(2,1)S(1)} %get-tuple-element.80), channel_id=1, source_target_pairs={{0,4},{2,6},{4,0},{6,2},{1,5},{3,7},{5,1},{7,3},{8,12},{10,14},{12... | collective-permute-start | bytes 1179656 | tf_op jit(solution)/shard_map/ppermute | solution.py:28
  133.5 18.9 %collective-permute-start.7 = (bf16[256,768]{1,0:T(8,128)(2,1)S(1)}, bf16[256,768]{1,0:T(8,128)(2,1)S(1)}, u32[]{:S(2)}, u32[]{:S(2)}) collective-permute-start(bf16[256,768]{1,0:T(8,128)(2,1)S(1)} %get-tuple-element.80), channel_id=1, source_target_pairs={{0,2},{2,4},{4,6},{6,0},{1,3},{3,5},{5,7},{7,1},{8,10},{10,12},{12... | collective-permute-start | bytes 1179656 | tf_op jit(solution)/shard_map/ppermute | solution.py:28
  152.5 0.8 copy-start.11
  154.2 107.9 %reduce-scatter.5.cloned.1.call-start = ((), (), s32[]{:S(2)}) async-start(), calls=%async_computation.5 | async-start | bytes 7077888 | tf_op jit(solution)/shard_map/reduce_scatter | solution.py:266
  154.3 1.0 copy-start.12
  155.5 37.0 %collective-permute-start.9 = (bf16[1024,768]{1,0:T(8,128)(2,1)S(1)}, bf16[1024,768]{1,0:T(8,128)(2,1)S(1)}, u32[]{:S(2)}, u32[]{:S(2)}) collective-permute-start(bf16[1024,768]{1,0:T(8,128)(2,1)S(1)} %constant_dynamic-slice_fusion.2), channel_id=1, source_target_pairs={{0,1},{1,0},{2,3},{3,2},{4,5},{5,4},{6,7},{7,6},{8,9},{9,8},{10,11... | collective-permute-start | bytes 4718600 | tf_op jit(solution)/shard_map/ppermute | solution.py:28
  192.6 1.2 copy-start.15
  195.2 1.9 copy-start.18
  197.1 4.7 %copy-start.6 = (bf16[2048,768]{1,0:T(8,128)(2,1)S(1)}, bf16[2048,768]{1,0:T(8,128)(2,1)}, u32[]{:S(2)}) copy-start(bf16[2048,768]{1,0:T(8,128)(2,1)} %pad_maximum_fusion.1) | copy-start | bytes 9437188
  205.0 3.5 %copy-start.8 = (bf16[2,1024,768]{2,1,0:T(8,128)(2,1)S(1)}, bf16[2,1024,768]{2,1,0:T(8,128)(2,1)}, u32[]{:S(2)}) copy-start(bf16[2,1024,768]{2,1,0:T(8,128)(2,1)} %copy-done.7) | copy-start | bytes 9437188
  205.0 3.8 %copy-start.14 = (bf16[2,1024,768]{2,1,0:T(8,128)(2,1)S(1)}, bf16[2,1024,768]{2,1,0:T(8,128)(2,1)}, u32[]{:S(2)}) copy-start(bf16[2,1024,768]{2,1,0:T(8,128)(2,1)} %all-gather.5.cloned.1.call-done) | copy-start | bytes 9437188
  216.2 2.1 collective-permute-start.11
  218.9 11.7 %collective-permute-start.12 = (bf16[96,768]{1,0:T(8,128)(2,1)S(1)}, bf16[96,768]{1,0:T(8,128)(2,1)}, u32[]{:S(2)}, u32[]{:S(2)}) collective-permute-start(bf16[96,768]{1,0:T(8,128)(2,1)S(1)} %get-tuple-element.108), channel_id=1, source_target_pairs={{0,32},{16,48},{32,0},{48,16},{1,33},{17,49},{33,1},{49,17},{2,34}... | collective-permute-start | bytes 442376 | tf_op jit(solution)/shard_map/ppermute | solution.py:28
  221.8 31.2 %collective-permute-start.13 = (bf16[96,768]{1,0:T(8,128)(2,1)S(1)}, bf16[96,768]{1,0:T(8,128)(2,1)S(1)}, u32[]{:S(2)}, u32[]{:S(2)}) collective-permute-start(bf16[96,768]{1,0:T(8,128)(2,1)S(1)} %get-tuple-element.107), channel_id=1, source_target_pairs={{0,16},{16,32},{32,48},{48,0},{1,17},{17,33},{33,49},{49,1},{2,18}... | collective-permute-start | bytes 442376 | tf_op jit(solution)/shard_map/ppermute | solution.py:28
  222.6 30.4 %collective-permute-start.14 = (bf16[96,768]{1,0:T(8,128)(2,1)S(1)}, bf16[96,768]{1,0:T(8,128)(2,1)S(1)}, u32[]{:S(2)}, u32[]{:S(2)}) collective-permute-start(bf16[96,768]{1,0:T(8,128)(2,1)S(1)} %get-tuple-element.109), channel_id=1, source_target_pairs={{0,48},{16,0},{32,16},{48,32},{1,49},{17,1},{33,17},{49,33},{2,50}... | collective-permute-start | bytes 442376 | tf_op jit(solution)/shard_map/ppermute | solution.py:28
  225.0 28.0 %collective-permute-start.15 = (bf16[2,96,768]{2,1,0:T(8,128)(2,1)S(1)}, bf16[2,96,768]{2,1,0:T(8,128)(2,1)S(1)}, u32[]{:S(2)}, u32[]{:S(2)}) collective-permute-start(bf16[2,96,768]{2,1,0:T(8,128)(2,1)S(1)} %get-tuple-element.110), channel_id=1, source_target_pairs={{0,4},{2,6},{4,0},{6,2},{1,5},{3,7},{5,1},{7,3},{8,12},{10,14},{12... | collective-permute-start | bytes 884744 | tf_op jit(solution)/shard_map/ppermute | solution.py:28
  227.1 26.0 %collective-permute-start.16 = (bf16[2,96,768]{2,1,0:T(8,128)(2,1)S(1)}, bf16[2,96,768]{2,1,0:T(8,128)(2,1)S(1)}, u32[]{:S(2)}, u32[]{:S(2)}) collective-permute-start(bf16[2,96,768]{2,1,0:T(8,128)(2,1)S(1)} %get-tuple-element.111), channel_id=1, source_target_pairs={{0,2},{2,4},{4,6},{6,0},{1,3},{3,5},{5,7},{7,1},{8,10},{10,12},{12... | collective-permute-start | bytes 884744 | tf_op jit(solution)/shard_map/ppermute | solution.py:28
  230.6 22.4 %collective-permute-start.17 = (bf16[2,96,768]{2,1,0:T(8,128)(2,1)S(1)}, bf16[2,96,768]{2,1,0:T(8,128)(2,1)S(1)}, u32[]{:S(2)}, u32[]{:S(2)}) collective-permute-start(bf16[2,96,768]{2,1,0:T(8,128)(2,1)S(1)} %get-tuple-element.112), channel_id=1, source_target_pairs={{0,6},{2,0},{4,2},{6,4},{1,7},{3,1},{5,3},{7,5},{8,14},{10,8},{12,... | collective-permute-start | bytes 884744 | tf_op jit(solution)/shard_map/ppermute | solution.py:28
  232.8 1.3 copy-start.3
  234.1 1.3 copy-start.5
  235.4 22.4 %copy-start.16 = (bf16[1024,768]{1,0:T(8,128)(2,1)S(1)}, bf16[1024,768]{1,0:T(8,128)(2,1)}, u32[]{:S(2)}) copy-start(bf16[1024,768]{1,0:T(8,128)(2,1)} %copy-done.15) | copy-start | bytes 4718596
  253.0 7.7 %copy-start.13 = (bf16[2,96,768]{2,1,0:T(8,128)(2,1)}, bf16[2,96,768]{2,1,0:T(8,128)(2,1)S(1)}, u32[]{:S(2)}) copy-start(bf16[2,96,768]{2,1,0:T(8,128)(2,1)S(1)} %collective-permute-done.16) | copy-start | bytes 884740
  253.1 13.3 %collective-permute-start.19 = (bf16[96,768]{1,0:T(8,128)(2,1)S(1)}, bf16[96,768]{1,0:T(8,128)(2,1)S(1)}, u32[]{:S(2)}, u32[]{:S(2)}) collective-permute-start(bf16[96,768]{1,0:T(8,128)(2,1)S(1)} %fusion.20), channel_id=1, source_target_pairs={{0,1},{1,0},{2,3},{3,2},{4,5},{5,4},{6,7},{7,6},{8,9},{9,8},{10,11... | collective-permute-start | bytes 442376 | tf_op jit(solution)/shard_map/ppermute | solution.py:28
  257.2 3.6 %copy-start.9 = (f32[768,768]{1,0:T(8,128)S(1)}, f32[768,768]{1,0:T(8,128)}, u32[]{:S(2)}) copy-start(f32[768,768]{1,0:T(8,128)} %fusion.13) | copy-start | bytes 7077892
  257.2 7.7 %collective-permute-start.18 = (bf16[48,768]{1,0:T(8,128)(2,1)S(1)}, bf16[48,768]{1,0:T(8,128)(2,1)}, u32[]{:S(2)}, u32[]{:S(2)}) collective-permute-start(bf16[48,768]{1,0:T(8,128)(2,1)S(1)} %fusion.21), channel_id=1, source_target_pairs={{0,64},{64,0},{1,65},{65,1},{2,66},{66,2},{3,67},{67,3},{4,68},{68... | collective-permute-start | bytes 221192 | tf_op jit(solution)/shard_map/ppermute | solution.py:28
  262.1 12.2 %copy-start.1 = (bf16[768,768]{1,0:T(8,128)(2,1)S(1)}, bf16[768,768]{1,0:T(8,128)(2,1)}, u32[]{:S(2)}) copy-start(bf16[768,768]{1,0:T(8,128)(2,1)} %param.11) | copy-start | bytes 3538948
  263.4 9.4 %collective-permute-start.10 = (bf16[256,768]{1,0:T(8,128)(2,1)S(1)}, bf16[256,768]{1,0:T(8,128)(2,1)S(1)}, u32[]{:S(2)}, u32[]{:S(2)}) collective-permute-start(bf16[256,768]{1,0:T(8,128)(2,1)S(1)} %bitcast.89), channel_id=1, source_target_pairs={{0,64},{64,0},{1,65},{65,1},{2,66},{66,2},{3,67},{67,3},{4,68},{68... | collective-permute-start | bytes 1179656 | tf_op jit(solution)/shard_map/ppermute | solution.py:28
Sparse Core Ops, SparseCore 0:
  10.3 44.7 all-gather.2
  65.0 37.8 reduce-scatter.2
  154.3 39.5 all-gather.4
  205.0 50.8 reduce-scatter.4
where the time goes:
time: 281 us
  waiting for transfers between devices  138 us (49%)
  starting transfers between devices  37.7 us (13%)
  matrix products  32.1 us (11%)
  Pallas kernels  27.6 us (10%)
  other arithmetic  17.6 us (6%)
  local copies, waits for them, and re-layouts  14.1 us (5%)
  between operations  14.1 us (5%)
    ppermute x20, waiting for transfers between devices, shift(): lax.ppermute(value, axis, [(i, (i + by) % size) for i in range(size)])  98.6 us
    all_gather x1, waiting for transfers between devices, shards(): lax.all_gather(jnp.stack(halves(tokens) + halves(cotangent)), ROW, axis=1...  39 us
    ppermute x20, starting transfers between devices, shift(): lax.ppermute(value, axis, [(i, (i + by) % size) for i in range(size)])  37.5 us
    dot_general x10, matrix products, matmul(): lax.dot_general(a, b, (((ca,), (cb,)), ((), ())), preferred_element_type=...  32.1 us
    pallas_call x4, Pallas kernels, call(): pl.pallas_call(kernel, out_shape=out_shape, grid_spec=pltpu.PrefetchScala...  27.6 us
    unnamed x44, local copies, waits for them, and re-layouts  9.33 us
  transfers between devices with their start and end apart: 24, of which 11 were waited for; matrix products, arithmetic and copies ran while one was open for 12% of the time, Pallas kernels for 10%

commit v1 on v0

--- a/solution.py
+++ b/solution.py
@@ -156,7 +156,7 @@
     return call(kernel, [0], (1,), [whole(shape)] * 2, [whole(shape)] * 5, [out] * 5, [], 0, left_basis, right_basis)
 
 
-def rotated_step(weight_grad, bases, first_moment, second_moment):
+def rotated_step(weight_grad, left, right, first_moment, second_moment):
     size = weight_grad.shape[0]
     parts = 3 if size % 384 == 0 else 1
     cut = size // parts
@@ -164,8 +164,8 @@
     def fine(a, b):
         return matmul(a[0], b[0]) + (matmul(a[0], b[1]) + matmul(a[1], b[0]))
 
-    def kernel(_, w_ref, l_ref, th_ref, tl_ref, rh_ref, rl_ref, m_ref, v_ref, *refs):
-        first_ref, second_ref, update_ref, high, low = refs
+    def kernel(_, w_ref, th_ref, tl_ref, rh_ref, rl_ref, m_ref, v_ref, *refs):
+        first_ref, second_ref, ratio_ref, high, low = refs
         step = pl.program_id(0)
 
         @pl.when(step == 0)
@@ -173,37 +173,27 @@
             turned = fine((th_ref[...], tl_ref[...]), split(w_ref[...]))
             high[...], low[...] = split(turned)
 
-        right = rh_ref[...], rl_ref[...]
-        rotated = fine((high[...], low[...]), right)
+        rotated = fine((high[...], low[...]), (rh_ref[...], rl_ref[...]))
         new_first = 0.9 * m_ref[...] + 0.1 * rotated
         new_second = 0.95 * v_ref[...] + 0.05 * rotated * rotated
         first_ref[...] = new_first
         second_ref[...] = new_second
-        ratio = new_first / (jnp.sqrt(new_second) + 1e-08)
-        back = matmul(l_ref[...], ratio.astype(bf16))
-        update = matmul(back.astype(bf16), right[0], 1, 1)
-
-        @pl.when(step == 0)
-        def _():
-            update_ref[...] = update
-
-        @pl.when(step > 0)
-        def _():
-            update_ref[...] += update
+        ratio_ref[...] = (new_first / (jnp.sqrt(new_second) + 1e-08)).astype(bf16)
 
     columns = pl.BlockSpec((size, cut), lambda i, _: (0, i))
-    out = jax.ShapeDtypeStruct((size, size), f32)
+    out = [jax.ShapeDtypeStruct((size, size), dtype) for dtype in (f32, f32, bf16)]
     return call(
         kernel,
         [0],
         (parts,),
-        [whole((size, size))] * 4 + [columns] * 4,
-        [columns, columns, whole((size, size))],
-        [out] * 3,
+        [whole((size, size))] * 3 + [columns] * 4,
+        [columns] * 3,
+        out,
         [pltpu.VMEM((size, size), bf16)] * 2,
-        16 * size**3,
+        12 * size**3,
         weight_grad,
-        *bases,
+        *left,
+        *right,
         first_moment,
         second_moment,
     )
@@ -249,20 +239,21 @@
     acts = ring_gather(act)
     grad = bf(add(parts[0], *back) * derivative)
     pair = shift(grad, "yh", 1)
-    acts, grad, pair = lax.optimization_barrier((acts, grad, pair))
+    act_own = jnp.zeros((half, width), bf16)
+    for k, piece in ((0, act), (1, acts[0]), (3, acts[2]), (2, acts[1])):
+        act_own = lax.dynamic_update_slice_in_dim(act_own, piece, ((x + k) % 4) * block, 0)
+    act_own, grad, pair = lax.optimization_barrier((act_own, grad, pair))
 
     grads = lax.all_gather(jnp.stack([grad, pair]), "x", axis=1, tiled=True)
-    turned = jnp.concatenate([act] + acts + [act] + acts[:2])
-    act_own = lax.dynamic_slice_in_dim(turned, ((4 - x) % 4) * block, half, 0)
     act_other = shift(act_own, "yh", 1)
     mixed_own = bf(matmul(act_own, w_out))
     out_grad = matmul(act_own, both[2], 0, 0)
     act_other, mixed_own, out_grad = lax.optimization_barrier((act_other, mixed_own, out_grad))
-    mixed = jnp.concatenate([mixed_own, bf(matmul(act_other, w_out))])
-    grads, mixed = lax.optimization_barrier((grads, mixed))
+    mixed_other = bf(matmul(act_other, w_out))
+    grads, mixed_other = lax.optimization_barrier((grads, mixed_other))
 
     carried = bf(matmul(grads.reshape(token_count, width), w_in_turned))
-    terms = jnp.concatenate([mixed, carried]).reshape(8, half // 2, width)
+    terms = jnp.concatenate([mixed_own, mixed_other, carried]).reshape(8, half // 2, width)
     sums = lax.psum_scatter(terms, ("z", "c"), scatter_dimension=1, tiled=True)
     terms, grads = lax.optimization_barrier((terms, grads))
     weight_grad = grad_scale * (matmul(line[:, :half], grads[0]) + matmul(line[:, half:], grads[1]))
@@ -270,27 +261,31 @@
     left_arrived = shift(left_send, "c", 1)
     left_arrived, right, weight_grad = lax.optimization_barrier((left_arrived, right, weight_grad))
     chip = core_sums(z, c, [], (left_keep, left_arrived))
-    chip_arrived = ring_send(chip, "z")
     right_arrived = ring_send(right, "x")
-    new_first, new_second, update = rotated_step(weight_grad, bases, first_moment, rotated_second_moment)
-    chip, chip_arrived, right_arrived, update, act_other = lax.optimization_barrier(
-        (chip, chip_arrived, right_arrived, update, act_other)
-    )
+    new_first, new_second, ratio = rotated_step(
+        weight_grad, bases[1:3], bases[3:], first_moment, rotated_second_moment
+    )
+    chip, right, right_arrived, ratio = lax.optimization_barrier((chip, right, right_arrived, ratio))
+
+    def along_yl(value, axis):
+        mine, theirs = (lax.dynamic_index_in_dim(value, at, axis, False) for at in (yl, 1 - yl))
+        return mine.reshape(-1, width), bf(theirs.reshape(-1, width))
 
     right_own = add(*[v[0] for v in (right[0], *right_arrived)])
     right_other = bf(add(*[v[1] for v in (right[0], *right_arrived)]))
     right_stat = add(right_own, shift(right_other, "yh", 1))
-    out_grad = bf(grad_scale * (out_grad + matmul(act_other, both[3], 0, 0)))
+    right_stat, ratio, act_other, chip, sums = lax.optimization_barrier((right_stat, ratio, act_other, chip, sums))
+
+    mine, theirs = along_yl(sums.reshape(4, 2, rows // 2, width), 1)
+    arrived = shift(theirs, "yl", 1)
+    chip_arrived = ring_send(chip, "z")
+    update = matmul(bf(matmul(bases[0], ratio)), bases[3], 1, 1)
+    chip_arrived, update, chip, act_other = lax.optimization_barrier((chip_arrived, update, chip, act_other))
     left = add(chip[0], *chip_arrived).reshape(2, -1, width)
-
-    def along_yl(value, axis):
-        mine, theirs = (lax.dynamic_index_in_dim(value, at, axis, False) for at in (yl, 1 - yl))
-        return mine.reshape(-1, width), bf(theirs.reshape(-1, width))
-
     left_mine, left_theirs = along_yl(left, 0)
     left_stat = add(left_mine, shift(left_theirs, "yl", 1))
-    mine, theirs = along_yl(sums.reshape(4, 2, rows // 2, width), 1)
-    last = bf(add(mine, shift(theirs, "yl", 1)))
+    out_grad = bf(grad_scale * (out_grad + matmul(act_other, both[3], 0, 0)))
+    last = bf(add(mine, arrived))
     mixed, carried = last[:rows], last[rows:]
 
     def ordered(value):

time: 281 us -> 278 us (0.989)
  matrix products: 32.1 us -> 41.9 us
  Pallas kernels: 27.6 us -> 21.8 us
  starting transfers between devices: 37.7 us -> 32.3 us
  waiting for transfers between devices: 138 us -> 134 us
  local copies, waits for them, and re-layouts: 14.1 us -> 17 us
    dot_general x10 -> x11, matrix products: 32.1 us -> 41.9 us  [matmul(): lax.dot_general(a, b, (((ca,), (cb,)), ((), ())), preferred_element_type=...]
    pallas_call x4, Pallas kernels: 27.6 us -> 21.8 us  [call(): pl.pallas_call(kernel, out_shape=out_shape, grid_spec=pltpu.PrefetchScala...]
    ppermute x20, starting transfers between devices: 37.5 us -> 32.1 us  [shift(): lax.ppermute(value, axis, [(i, (i + by) % size) for i in range(size)])]
    ppermute x20, waiting for transfers between devices: 98.6 us -> 94.1 us  [shift(): lax.ppermute(value, axis, [(i, (i + by) % size) for i in range(size)])]
    dynamic_update_slice x0 -> x4, local copies, waits for them, and re-layouts: none -> 3.08 us  [shards(): lax.dynamic_update_slice_in_dim(act_own, piece, (x + k) % 4 * block, 0)]
    unnamed x44 -> x52, local copies, waits for them, and re-layouts: 9.33 us -> 6.93 us
  transfers between devices with their start and end apart: 24 -> 24, of which waited for: 11 -> 11; matrix products, arithmetic and copies ran while one was open for 12% -> 16% of each run, Pallas kernels for 10% -> 8%
where the time goes in v1:
time: 278 us; the launch traced here: 277 us
  waiting for transfers between devices  134 us (48%)
  matrix products  41.9 us (15%)
  starting transfers between devices  32.3 us (12%)
  Pallas kernels  21.8 us (8%)
  local copies, waits for them, and re-layouts  17 us (6%)
  other arithmetic  15.9 us (6%)
  between operations  14 us (5%)
    ppermute x20, waiting for transfers between devices, shift(): lax.ppermute(value, axis, [(i, (i + by) % size) for i in range(size)])  94.1 us
    dot_general x11, matrix products, matmul(): lax.dot_general(a, b, (((ca,), (cb,)), ((), ())), preferred_element_type=...  41.9 us
    all_gather x1, waiting for transfers between devices, shards(): lax.all_gather(jnp.stack(halves(tokens) + halves(cotangent)), ROW, axis=1...  40 us
    ppermute x20, starting transfers between devices, shift(): lax.ppermute(value, axis, [(i, (i + by) % size) for i in range(size)])  32.1 us
    pallas_call x4, Pallas kernels, call(): pl.pallas_call(kernel, out_shape=out_shape, grid_spec=pltpu.PrefetchScala...  21.8 us
    unnamed x52, local copies, waits for them, and re-layouts  6.93 us
  transfers between devices with their start and end apart: 24, of which 11 were waited for; matrix products, arithmetic and copies ran while one was open for 16% of the time, Pallas kernels for 8%

profile of v1, /device:TPU:2, one launch (start us, length us, event | category | flops | bytes accessed | tf_op | source)
XLA Modules:
  0.0 277.0 jit_solution(5381411553599615653)
XLA Ops:
  7.2 1.2 constant_dynamic-slice_fusion.7
  9.3 4.8 %shard_map.143 = (bf16[768,768]{1,0:T(8,128)(2,1)S(1)}, bf16[768,768]{1,0:T(8,128)(2,1)S(1)}, bf16[768,768]{1,0:T(8,128)(2,1)S(1)}, bf16[768,768]{1,0:T(8,128)(2,1)}, bf16[768,768]{1,0:T(8,128)(2,1)}) custom-call(s32[1]{0:T(128)} %constant.90.clone.1._, f32[768,768]{1,0:T(8,128)} %left_ref.1, f32[768,768]{1,0:T(8,128)} %right_ref.1), custom_call_target="tpu_custom_call" | custom-call | bytes 10616832 | tf_op jit(solution)/shard_map/pallas_call | solution.py:58
  15.1 40.0 %all-gather.3.cloned.1.call-done = bf16[4,1024,768]{2,1,0:T(8,128)(2,1)} async-done(((bf16[4,64,768]{2,1,0:T(8,128)(2,1)}), bf16[4,1024,768]{2,1,0:T(8,128)(2,1)}) %all-gather.3.cloned.1.call-update) | async-done | bytes 6291472 | tf_op jit(solution)/shard_map/all_gather | solution.py:218
  55.1 4.1 %convolution_convert_fusion.4 = bf16[1024,768]{1,0:T(8,128)(2,1)} fusion(bf16[768,768]{0,1:T(8,128)(2,1)S(1)} %bitcast.79, bf16[4,1024,768]{2,1,0:T(8,128)(2,1)} %all-gather.3.cloned.1.call-done), kind=kOutput, calls=%fused_computation.8 | convolution fusion | flops 1208745984 | bytes 4325376 | tf_op jit(solution)/shard_map/dot_general | solution.py:39
  59.4 1.4 copy-done.25
  60.8 4.0 %convolution_convert_fusion.1 = bf16[2048,768]{1,0:T(8,128)(2,1)} fusion(bf16[2048,768]{1,0:T(8,128)(2,1)S(1)} %bitcast.83, bf16[768,768]{1,0:T(8,128)(2,1)S(1)} %copy-done.25), kind=kOutput, calls=%fused_computation.2 | convolution fusion | flops 2417491968 | bytes 7471104 | tf_op jit(solution)/shard_map/dot_general | solution.py:39
  64.9 2.9 %collective-permute-start = (bf16[1024,768]{1,0:T(8,128)(2,1)}, bf16[1024,768]{1,0:T(8,128)(2,1)}, u32[]{:S(2)}, u32[]{:S(2)}) collective-permute-start(bf16[1024,768]{1,0:T(8,128)(2,1)} %convolution_convert_fusion.4), channel_id=1, source_target_pairs={{0,1},{1,0},{2,3},{3,2},{4,5},{5,4},{6,7},{7,6},{8,9},{9,8},{10,11... | collective-permute-start | bytes 4718600 | tf_op jit(solution)/shard_map/ppermute | solution.py:28
  67.8 2.8 %fusion.14 = f32[1024,768]{1,0:T(8,128)S(1)} fusion(bf16[768,768]{0,1:T(8,128)(2,1)S(1)} %bitcast.78, bf16[4,1024,768]{2,1,0:T(8,128)(2,1)} %all-gather.3.cloned.1.call-done), kind=kOutput, calls=%fused_computation.22 | convolution fusion | flops 1207959552 | bytes 5898240 | tf_op jit(solution)/shard_map/dot_general | solution.py:39
  70.7 32.7 %collective-permute-done = bf16[1024,768]{1,0:T(8,128)(2,1)} collective-permute-done((bf16[1024,768]{1,0:T(8,128)(2,1)}, bf16[1024,768]{1,0:T(8,128)(2,1)}, u32[]{:S(2)}, u32[]{:S(2)}) %collective-permute-start) | collective-permute-done | bytes 1572896 | tf_op jit(solution)/shard_map/ppermute | solution.py:28
  103.3 1.9 add_convert_fusion
  105.2 1.2 constant_dynamic-slice_fusion.2
  107.5 2.9 %collective-permute-start.1 = (bf16[256,768]{1,0:T(8,128)(2,1)S(1)}, bf16[256,768]{1,0:T(8,128)(2,1)S(1)}, u32[]{:S(2)}, u32[]{:S(2)}) collective-permute-start(bf16[256,768]{1,0:T(8,128)(2,1)S(1)} %slice_bitcast_fusion.6), channel_id=1, source_target_pairs={{0,1},{1,0},{2,3},{3,2},{4,5},{5,4},{6,7},{7,6},{8,9},{9,8},{10,11... | collective-permute-start | bytes 1179656 | tf_op jit(solution)/shard_map/ppermute | solution.py:28
  110.4 2.1 collective-permute-start.2
  112.5 2.0 collective-permute-start.4
  114.5 5.0 %collective-permute-done.1 = bf16[256,768]{1,0:T(8,128)(2,1)S(1)} collective-permute-done((bf16[256,768]{1,0:T(8,128)(2,1)S(1)}, bf16[256,768]{1,0:T(8,128)(2,1)S(1)}, u32[]{:S(2)}, u32[]{:S(2)}) %collective-permute-start.1) | collective-permute-done | bytes 393248 | tf_op jit(solution)/shard_map/ppermute | solution.py:28
  119.5 1.4 fusion.19
  120.9 3.3 %collective-permute-done.2 = bf16[256,768]{1,0:T(8,128)(2,1)S(1)} collective-permute-done((bf16[256,768]{1,0:T(8,128)(2,1)}, bf16[256,768]{1,0:T(8,128)(2,1)S(1)}, u32[]{:S(2)}, u32[]{:S(2)}) %collective-permute-start.2) | collective-permute-done | bytes 393248 | tf_op jit(solution)/shard_map/ppermute | solution.py:28
  124.2 6.6 %collective-permute-done.3 = bf16[256,768]{1,0:T(8,128)(2,1)S(1)} collective-permute-done((bf16[256,768]{1,0:T(8,128)(2,1)}, bf16[256,768]{1,0:T(8,128)(2,1)S(1)}, u32[]{:S(2)}, u32[]{:S(2)}) %collective-permute-start.3) | collective-permute-done | bytes 393248 | tf_op jit(solution)/shard_map/ppermute | solution.py:28
  131.3 1.5 collective-permute-start.6
  132.8 3.2 %collective-permute-start.7 = (bf16[256,768]{1,0:T(8,128)(2,1)S(1)}, bf16[256,768]{1,0:T(8,128)(2,1)S(1)}, u32[]{:S(2)}, u32[]{:S(2)}) collective-permute-start(bf16[256,768]{1,0:T(8,128)(2,1)S(1)} %get-tuple-element.93), channel_id=1, source_target_pairs={{0,4},{2,6},{4,0},{6,2},{1,5},{3,7},{5,1},{7,3},{8,12},{10,14},{12... | collective-permute-start | bytes 1179656 | tf_op jit(solution)/shard_map/ppermute | solution.py:28
  137.0 1.2 broadcast_in_dim.3
  139.0 3.0 %collective-permute-done.5 = bf16[256,768]{1,0:T(8,128)(2,1)S(1)} collective-permute-done((bf16[256,768]{1,0:T(8,128)(2,1)S(1)}, bf16[256,768]{1,0:T(8,128)(2,1)S(1)}, u32[]{:S(2)}, u32[]{:S(2)}) %collective-permute-start.5) | collective-permute-done | bytes 393248 | tf_op jit(solution)/shard_map/ppermute | solution.py:28
  142.8 1.1 collective-permute-done.6
  144.7 5.8 %collective-permute-done.7 = bf16[256,768]{1,0:T(8,128)(2,1)S(1)} collective-permute-done((bf16[256,768]{1,0:T(8,128)(2,1)S(1)}, bf16[256,768]{1,0:T(8,128)(2,1)S(1)}, u32[]{:S(2)}, u32[]{:S(2)}) %collective-permute-start.7) | collective-permute-done | bytes 393248 | tf_op jit(solution)/shard_map/ppermute | solution.py:28
  153.2 4.0 %convolution_convert_fusion.3 = bf16[1024,768]{1,0:T(8,128)(2,1)} fusion(bf16[1024,768]{1,0:T(8,128)(2,1)} %constant_dynamic-update-slice_fusion, bf16[768,768]{1,0:T(8,128)(2,1)S(1)} %copy-done), kind=kOutput, calls=%fused_computation.7 | convolution fusion | flops 1208745984 | bytes 4325376 | tf_op jit(solution)/shard_map/dot_general | solution.py:39
  157.2 4.8 %fusion.13 = f32[768,768]{1,0:T(8,128)} fusion(bf16[1024,768]{1,0:T(8,128)(2,1)} %constant_dynamic-update-slice_fusion, bf16[4,1024,768]{2,1,0:T(8,128)(2,1)} %all-gather.3.cloned.1.call-done), kind=kOutput, calls=%fused_computation.21 | convolution fusion | flops 1207959552 | bytes 5505024 | tf_op jit(solution)/shard_map/dot_general | solution.py:39
  162.0 28.1 %collective-permute-done.9 = bf16[1024,768]{1,0:T(8,128)(2,1)S(1)} collective-permute-done((bf16[1024,768]{1,0:T(8,128)(2,1)}, bf16[1024,768]{1,0:T(8,128)(2,1)S(1)}, u32[]{:S(2)}, u32[]{:S(2)}) %collective-permute-start.9) | collective-permute-done | bytes 1572896 | tf_op jit(solution)/shard_map/ppermute | solution.py:28
  190.1 1.2 copy-done.24
  191.3 2.5 convolution_convert_fusion.2
  193.8 5.0 %convolution_convert_fusion = bf16[2048,768]{1,0:T(8,128)(2,1)S(1)} fusion(bf16[2048,768]{1,0:T(8,128)(2,1)} %bitcast.94, bf16[768,768]{0,1:T(8,128)(2,1)} %bitcast.95), kind=kOutput, calls=%fused_computation.1 | convolution fusion | flops 2417491968 | bytes 7471104 | tf_op jit(solution)/shard_map/dot_general | solution.py:39
  198.9 3.3 %pad_maximum_fusion = bf16[4096,768]{1,0:T(8,128)(2,1)} fusion(bf16[2048,768]{1,0:T(8,128)(2,1)S(1)} %convolution_convert_fusion, bf16[1024,768]{1,0:T(8,128)(2,1)S(1)} %copy-done.16, bf16[1024,768]{1,0:T(8,128)(2,1)S(1)} %copy-done.15), kind=kLoop, calls=%fused_computation | loop fusion | flops 18874368 | bytes 12582912 | tf_op jit(solution)/shard_map/concatenate | solution.py:256
  202.2 3.5 %fusion = f32[768,768]{1,0:T(8,128)S(1)} fusion(bf16[2,1024,768]{2,1,0:T(8,128)(2,1)} %all-gather.5.cloned.1.call-done, bf16[768,2048]{0,1:T(8,128)(2,1)} %bitcast.84), kind=kOutput, calls=%fused_computation.11 | convolution fusion | flops 1207959552 | bytes 5505024 | tf_op jit(solution)/shard_map/dot_general | solution.py:39
  206.0 2.9 %add_multiply_fusion.weight_ref.w_ref = f32[768,768]{1,0:T(8,128)} fusion(f32[768,768]{1,0:T(8,128)S(1)} %fusion, bf16[2,1024,768]{2,1,0:T(8,128)(2,1)S(1)} %copy-done.23, bf16[768,2048]{0,1:T(8,128)(2,1)S(1)} %bitcast.85), kind=kOutput, calls=%fused_computation.5 | convolution fusion | flops 1209139200 | bytes 7864320 | tf_op jit(solution)/shard_map/dot_general | solution.py:39
  209.0 4.5 %shard_map.144 = (bf16[4,2,48,768]{3,2,1,0:T(8,128)(2,1)S(1)}, bf16[4,2,48,768]{3,2,1,0:T(8,128)(2,1)S(1)}, bf16[2,96,768]{2,1,0:T(8,128)(2,1)S(1)}, bf16[2,96,7...) custom-call(s32[4]{0:T(128)S(1)} %pad_add_fusion.1.at, ...), custom_call_target="tpu_custom_call" | custom-call | flops 1811939328 | bytes 4718592 | tf_op jit(solution)/shard_map/pallas_call | solution.py:58
  213.6 1.9 collective-permute-done.10
  215.5 4.5 %collective-permute-start.11 = (bf16[2,96,768]{2,1,0:T(8,128)(2,1)S(1)}, bf16[2,96,768]{2,1,0:T(8,128)(2,1)S(1)}, u32[]{:S(2)}, u32[]{:S(2)}) collective-permute-start(bf16[2,96,768]{2,1,0:T(8,128)(2,1)S(1)} %get-tuple-element.121), channel_id=1, source_target_pairs={{0,4},{2,6},{4,0},{6,2},{1,5},{3,7},{5,1},{7,3},{8,12},{10,14},{12... | collective-permute-start | bytes 884744 | tf_op jit(solution)/shard_map/ppermute | solution.py:28
  221.0 1.1 collective-permute-start.13
  224.1 11.9 %shard_map.146 = (f32[768,768]{1,0:T(8,128)}, f32[768,768]{1,0:T(8,128)}, bf16[768,768]{1,0:T(8,128)(2,1)S(1)}) custom-call(s32[1]{0:T(128)} %constant.90.clone.1._, f32[768,768]{1,0:T(8,128)} %add_multiply_fusion.weight_ref.w_ref, bf16[768,768]{1,0:T(8,128)(2,1)S(1)} %get-tuple-element.124.th_ref, bf16[768,768]{1,0:T(8,128)(2,1)S(1)} %copy-done.3, ...), custom_call_target="tpu_custom_call" | custom-call | flops 5435817984 | bytes 17694720 | tf_op jit(solution)/shard_map/pallas_call | solution.py:58
  238.8 6.5 %collective-permute-done.14 = bf16[96,768]{1,0:T(8,128)(2,1)S(1)} collective-permute-done((bf16[96,768]{1,0:T(8,128)(2,1)}, bf16[96,768]{1,0:T(8,128)(2,1)S(1)}, u32[]{:S(2)}, u32[]{:S(2)}) %collective-permute-start.14) | collective-permute-done | bytes 147488 | tf_op jit(solution)/shard_map/ppermute | solution.py:28
  245.3 1.9 bitcast_add_fusion
  247.2 2.9 %collective-permute-start.16 = (bf16[96,768]{1,0:T(8,128)(2,1)S(1)}, bf16[96,768]{1,0:T(8,128)(2,1)S(1)}, u32[]{:S(2)}, u32[]{:S(2)}) collective-permute-start(bf16[96,768]{1,0:T(8,128)(2,1)S(1)} %copy-done.9), channel_id=1, source_target_pairs={{0,32},{16,48},{32,0},{48,16},{1,33},{17,49},{33,1},{49,17},{2,34}... | collective-permute-start | bytes 442376 | tf_op jit(solution)/shard_map/ppermute | solution.py:28
  250.7 2.6 collective-permute-start.18
  253.3 2.0 constant_dynamic-slice_fusion.1
  255.5 4.8 %fusion.15 = f32[768,768]{1,0:T(8,128)} fusion(bf16[768,768]{1,0:T(8,128)(2,1)} %get-tuple-element.126.rh_ref, bf16[768,768]{1,0:T(8,128)(2,1)S(1)} %get-tuple-element.143, bf16[768,768]{1,0:T(8,128)(2,1)S(1)} %copy-done.11), kind=kOutput, calls=%fused_computation.24 | convolution fusion | flops 1812529152 | bytes 5898240 | tf_op jit(solution)/shard_map/dot_general | solution.py:39
  260.4 1.9 collective-permute-start.19
  262.4 3.5 %fusion.12 = f32[768,768]{1,0:T(8,128)S(1)} fusion(bf16[1024,768]{1,0:T(8,128)(2,1)} %copy-done.24, bf16[4,1024,768]{2,1,0:T(8,128)(2,1)} %all-gather.3.cloned.1.call-done), kind=kOutput, calls=%fused_computation.20 | convolution fusion | flops 1207959552 | bytes 5505024 | tf_op jit(solution)/shard_map/dot_general | solution.py:39
  265.9 1.4 multiply_convert_fusion
  268.0 1.1 fusion.20
  (99 shorter events, 19.0 us)
Async XLA Ops:
  7.2 7.9 %copy-start = (bf16[768,768]{1,0:T(8,128)(2,1)S(1)}, bf16[768,768]{1,0:T(8,128)(2,1)}, u32[]{:S(2)}) copy-start(bf16[768,768]{1,0:T(8,128)(2,1)} %param.11) | copy-start | bytes 3538948
  7.2 47.9 %all-gather.3.cloned.1.call-start = ((), (), s32[]{:S(2)}) async-start(), calls=%async_computation.2 | async-start | bytes 6684672 | tf_op jit(solution)/shard_map/all_gather | solution.py:218
  9.2 97.2 %reduce-scatter.3.cloned.1.call-start = ((), (), s32[]{:S(2)}) async-start(), calls=%async_computation.3 | async-start | bytes 3932160 | tf_op jit(solution)/shard_map/reduce_scatter | solution.py:227
  14.0 1.0 copy-start.2
  55.1 4.1 %copy-start.17 = (bf16[4,1024,768]{2,1,0:T(8,128)(2,1)S(1)}, bf16[4,1024,768]{2,1,0:T(8,128)(2,1)}, u32[]{:S(2)}) copy-start(bf16[4,1024,768]{2,1,0:T(8,128)(2,1)} %all-gather.3.cloned.1.call-done) | copy-start | bytes 18874372
  59.2 1.6 copy-start.25
  59.4 5.4 %copy-start.12 = (bf16[2,1024,768]{2,1,0:T(8,128)(2,1)}, bf16[2,1024,768]{2,1,0:T(8,128)(2,1)S(1)}, u32[]{:S(2)}) copy-start(bf16[2,1024,768]{2,1,0:T(8,128)(2,1)S(1)} %slice.95) | copy-start | bytes 9437188
  64.8 129.0 %all-gather.5.cloned.1.call-start = ((), (), s32[]{:S(2)}) async-start(), calls=%async_computation.4 | async-start | bytes 3932160 | tf_op jit(solution)/shard_map/all_gather | solution.py:247
  64.9 38.4 %collective-permute-start = (bf16[1024,768]{1,0:T(8,128)(2,1)}, bf16[1024,768]{1,0:T(8,128)(2,1)}, u32[]{:S(2)}, u32[]{:S(2)}) collective-permute-start(bf16[1024,768]{1,0:T(8,128)(2,1)} %convolution_convert_fusion.4), channel_id=1, source_target_pairs={{0,1},{1,0},{2,3},{3,2},{4,5},{5,4},{6,7},{7,6},{8,9},{9,8},{10,11... | collective-permute-start | bytes 4718600 | tf_op jit(solution)/shard_map/ppermute | solution.py:28
  106.4 29.7 %copy-start.19 = (bf16[256,768]{1,0:T(8,128)(2,1)S(1)}, bf16[256,768]{1,0:T(8,128)(2,1)}, u32[]{:S(2)}) copy-start(bf16[256,768]{1,0:T(8,128)(2,1)} %get-tuple-element.94) | copy-start | bytes 1179652
  107.5 12.0 %collective-permute-start.1 = (bf16[256,768]{1,0:T(8,128)(2,1)S(1)}, bf16[256,768]{1,0:T(8,128)(2,1)S(1)}, u32[]{:S(2)}, u32[]{:S(2)}) collective-permute-start(bf16[256,768]{1,0:T(8,128)(2,1)S(1)} %slice_bitcast_fusion.6), channel_id=1, source_target_pairs={{0,1},{1,0},{2,3},{3,2},{4,5},{5,4},{6,7},{7,6},{8,9},{9,8},{10,11... | collective-permute-start | bytes 1179656 | tf_op jit(solution)/shard_map/ppermute | solution.py:28
  110.4 13.8 %collective-permute-start.2 = (bf16[256,768]{1,0:T(8,128)(2,1)}, bf16[256,768]{1,0:T(8,128)(2,1)S(1)}, u32[]{:S(2)}, u32[]{:S(2)}) collective-permute-start(bf16[256,768]{1,0:T(8,128)(2,1)} %get-tuple-element.157), channel_id=1, source_target_pairs={{0,4},{2,6},{4,0},{6,2},{1,5},{3,7},{5,1},{7,3},{8,12},{10,14},{12... | collective-permute-start | bytes 1179656 | tf_op jit(solution)/shard_map/ppermute | solution.py:28
  112.5 18.3 %collective-permute-start.3 = (bf16[256,768]{1,0:T(8,128)(2,1)}, bf16[256,768]{1,0:T(8,128)(2,1)S(1)}, u32[]{:S(2)}, u32[]{:S(2)}) collective-permute-start(bf16[256,768]{1,0:T(8,128)(2,1)} %get-tuple-element.158), channel_id=1, source_target_pairs={{0,2},{2,4},{4,6},{6,0},{1,3},{3,5},{5,7},{7,1},{8,10},{10,12},{12... | collective-permute-start | bytes 1179656 | tf_op jit(solution)/shard_map/ppermute | solution.py:28
  112.5 18.3 %collective-permute-start.4 = (bf16[256,768]{1,0:T(8,128)(2,1)}, bf16[256,768]{1,0:T(8,128)(2,1)S(1)}, u32[]{:S(2)}, u32[]{:S(2)}) collective-permute-start(bf16[256,768]{1,0:T(8,128)(2,1)} %get-tuple-element.156), channel_id=1, source_target_pairs={{0,6},{2,0},{4,2},{6,4},{1,7},{3,1},{5,3},{7,5},{8,14},{10,8},{12,... | collective-permute-start | bytes 1179656 | tf_op jit(solution)/shard_map/ppermute | solution.py:28
  130.8 11.3 %collective-permute-start.5 = (bf16[256,768]{1,0:T(8,128)(2,1)S(1)}, bf16[256,768]{1,0:T(8,128)(2,1)S(1)}, u32[]{:S(2)}, u32[]{:S(2)}) collective-permute-start(bf16[256,768]{1,0:T(8,128)(2,1)S(1)} %get-tuple-element.93), channel_id=1, source_target_pairs={{0,6},{2,0},{4,2},{6,4},{1,7},{3,1},{5,3},{7,5},{8,14},{10,8},{12,... | collective-permute-start | bytes 1179656 | tf_op jit(solution)/shard_map/ppermute | solution.py:28
  131.3 12.6 %collective-permute-start.6 = (bf16[256,768]{1,0:T(8,128)(2,1)S(1)}, bf16[256,768]{1,0:T(8,128)(2,1)S(1)}, u32[]{:S(2)}, u32[]{:S(2)}) collective-permute-start(bf16[256,768]{1,0:T(8,128)(2,1)S(1)} %get-tuple-element.93), channel_id=1, source_target_pairs={{0,2},{2,4},{4,6},{6,0},{1,3},{3,5},{5,7},{7,1},{8,10},{10,12},{12... | collective-permute-start | bytes 1179656 | tf_op jit(solution)/shard_map/ppermute | solution.py:28
  132.8 17.7 %collective-permute-start.7 = (bf16[256,768]{1,0:T(8,128)(2,1)S(1)}, bf16[256,768]{1,0:T(8,128)(2,1)S(1)}, u32[]{:S(2)}, u32[]{:S(2)}) collective-permute-start(bf16[256,768]{1,0:T(8,128)(2,1)S(1)} %get-tuple-element.93), channel_id=1, source_target_pairs={{0,4},{2,6},{4,0},{6,2},{1,5},{3,7},{5,1},{7,3},{8,12},{10,14},{12... | collective-permute-start | bytes 1179656 | tf_op jit(solution)/shard_map/ppermute | solution.py:28
  136.3 15.0 %collective-permute-start.8 = (bf16[256,768]{1,0:T(8,128)(2,1)S(1)}, bf16[256,768]{1,0:T(8,128)(2,1)S(1)}, u32[]{:S(2)}, u32[]{:S(2)}) collective-permute-start(bf16[256,768]{1,0:T(8,128)(2,1)S(1)} %multiply_convert_fusion.1), channel_id=1, source_target_pairs={{0,1},{1,0},{2,3},{3,2},{4,5},{5,4},{6,7},{7,6},{8,9},{9,8},{10,11... | collective-permute-start | bytes 1179656 | tf_op jit(solution)/shard_map/ppermute | solution.py:28
  152.3 94.9 %reduce-scatter.5.cloned.1.call-start = ((), (), s32[]{:S(2)}) async-start(), calls=%async_computation.5 | async-start | bytes 7077888 | tf_op jit(solution)/shard_map/reduce_scatter | solution.py:257
  152.3 37.8 %collective-permute-start.9 = (bf16[1024,768]{1,0:T(8,128)(2,1)}, bf16[1024,768]{1,0:T(8,128)(2,1)S(1)}, u32[]{:S(2)}, u32[]{:S(2)}) collective-permute-start(bf16[1024,768]{1,0:T(8,128)(2,1)} %constant_dynamic-update-slice_fusion), channel_id=1, source_target_pairs={{0,1},{1,0},{2,3},{3,2},{4,5},{5,4},{6,7},{7,6},{8,9},{9,8},{10,11... | collective-permute-start | bytes 4718600 | tf_op jit(solution)/shard_map/ppermute | solution.py:28
  190.1 1.2 copy-start.24
  193.8 5.0 %copy-start.15 = (bf16[1024,768]{1,0:T(8,128)(2,1)S(1)}, bf16[1024,768]{1,0:T(8,128)(2,1)}, u32[]{:S(2)}) copy-start(bf16[1024,768]{1,0:T(8,128)(2,1)} %convolution_convert_fusion.3) | copy-start | bytes 4718596
  193.8 5.0 %copy-start.16 = (bf16[1024,768]{1,0:T(8,128)(2,1)S(1)}, bf16[1024,768]{1,0:T(8,128)(2,1)}, u32[]{:S(2)}) copy-start(bf16[1024,768]{1,0:T(8,128)(2,1)} %convolution_convert_fusion.2) | copy-start | bytes 4718596
  202.2 3.5 %copy-start.13 = (bf16[2,1024,768]{2,1,0:T(8,128)(2,1)S(1)}, bf16[2,1024,768]{2,1,0:T(8,128)(2,1)}, u32[]{:S(2)}) copy-start(bf16[2,1024,768]{2,1,0:T(8,128)(2,1)} %copy-done.12) | copy-start | bytes 9437188
  202.2 3.8 %copy-start.23 = (bf16[2,1024,768]{2,1,0:T(8,128)(2,1)S(1)}, bf16[2,1024,768]{2,1,0:T(8,128)(2,1)}, u32[]{:S(2)}) copy-start(bf16[2,1024,768]{2,1,0:T(8,128)(2,1)} %all-gather.5.cloned.1.call-done) | copy-start | bytes 9437188
  209.0 15.1 %copy-start.3 = (bf16[768,768]{1,0:T(8,128)(2,1)S(1)}, bf16[768,768]{1,0:T(8,128)(2,1)}, u32[]{:S(2)}) copy-start(bf16[768,768]{1,0:T(8,128)(2,1)} %copy-done.2) | copy-start | bytes 3538948
  213.4 2.1 collective-permute-start.10
  215.5 21.5 %collective-permute-start.11 = (bf16[2,96,768]{2,1,0:T(8,128)(2,1)S(1)}, bf16[2,96,768]{2,1,0:T(8,128)(2,1)S(1)}, u32[]{:S(2)}, u32[]{:S(2)}) collective-permute-start(bf16[2,96,768]{2,1,0:T(8,128)(2,1)S(1)} %get-tuple-element.121), channel_id=1, source_target_pairs={{0,4},{2,6},{4,0},{6,2},{1,5},{3,7},{5,1},{7,3},{8,12},{10,14},{12... | collective-permute-start | bytes 884744 | tf_op jit(solution)/shard_map/ppermute | solution.py:28
  220.1 17.0 %collective-permute-start.12 = (bf16[2,96,768]{2,1,0:T(8,128)(2,1)S(1)}, bf16[2,96,768]{2,1,0:T(8,128)(2,1)S(1)}, u32[]{:S(2)}, u32[]{:S(2)}) collective-permute-start(bf16[2,96,768]{2,1,0:T(8,128)(2,1)S(1)} %get-tuple-element.120), channel_id=1, source_target_pairs={{0,2},{2,4},{4,6},{6,0},{1,3},{3,5},{5,7},{7,1},{8,10},{10,12},{12... | collective-permute-start | bytes 884744 | tf_op jit(solution)/shard_map/ppermute | solution.py:28
  221.0 16.1 %collective-permute-start.13 = (bf16[2,96,768]{2,1,0:T(8,128)(2,1)S(1)}, bf16[2,96,768]{2,1,0:T(8,128)(2,1)S(1)}, u32[]{:S(2)}, u32[]{:S(2)}) collective-permute-start(bf16[2,96,768]{2,1,0:T(8,128)(2,1)S(1)} %get-tuple-element.122), channel_id=1, source_target_pairs={{0,6},{2,0},{4,2},{6,4},{1,7},{3,1},{5,3},{7,5},{8,14},{10,8},{12,... | collective-permute-start | bytes 884744 | tf_op jit(solution)/shard_map/ppermute | solution.py:28
  224.1 11.9 %copy-start.4 = (bf16[96,768]{1,0:T(8,128)(2,1)}, bf16[96,768]{1,0:T(8,128)(2,1)S(1)}, u32[]{:S(2)}) copy-start(bf16[96,768]{1,0:T(8,128)(2,1)S(1)} %get-tuple-element.142) | copy-start | bytes 442372
  236.0 1.0 copy-start.10
  237.0 10.2 %copy-start.9 = (bf16[96,768]{1,0:T(8,128)(2,1)S(1)}, bf16[96,768]{1,0:T(8,128)(2,1)}, u32[]{:S(2)}) copy-start(bf16[96,768]{1,0:T(8,128)(2,1)} %copy-done.8) | copy-start | bytes 442372
  237.0 13.1 %copy-start.7 = (bf16[96,768]{1,0:T(8,128)(2,1)S(1)}, bf16[96,768]{1,0:T(8,128)(2,1)}, u32[]{:S(2)}) copy-start(bf16[96,768]{1,0:T(8,128)(2,1)} %copy-done.6) | copy-start | bytes 442372
  237.0 0.7 copy-start.20
  237.0 13.7 %copy-start.5 = (bf16[96,768]{1,0:T(8,128)(2,1)S(1)}, bf16[96,768]{1,0:T(8,128)(2,1)}, u32[]{:S(2)}) copy-start(bf16[96,768]{1,0:T(8,128)(2,1)} %copy-done.4) | copy-start | bytes 442372
  237.1 1.4 copy-start.21
  237.1 1.4 copy-start.22
  237.7 17.8 %copy-start.11 = (bf16[768,768]{1,0:T(8,128)(2,1)S(1)}, bf16[768,768]{1,0:T(8,128)(2,1)}, u32[]{:S(2)}) copy-start(bf16[768,768]{1,0:T(8,128)(2,1)} %copy-done.10) | copy-start | bytes 3538948
  238.5 6.9 %collective-permute-start.14 = (bf16[96,768]{1,0:T(8,128)(2,1)}, bf16[96,768]{1,0:T(8,128)(2,1)S(1)}, u32[]{:S(2)}, u32[]{:S(2)}) collective-permute-start(bf16[96,768]{1,0:T(8,128)(2,1)} %fusion.21), channel_id=1, source_target_pairs={{0,1},{1,0},{2,3},{3,2},{4,5},{5,4},{6,7},{7,6},{8,9},{9,8},{10,11... | collective-permute-start | bytes 442376 | tf_op jit(solution)/shard_map/ppermute | solution.py:28
  247.2 13.1 %collective-permute-start.16 = (bf16[96,768]{1,0:T(8,128)(2,1)S(1)}, bf16[96,768]{1,0:T(8,128)(2,1)S(1)}, u32[]{:S(2)}, u32[]{:S(2)}) collective-permute-start(bf16[96,768]{1,0:T(8,128)(2,1)S(1)} %copy-done.9), channel_id=1, source_target_pairs={{0,32},{16,48},{32,0},{48,16},{1,33},{17,49},{33,1},{49,17},{2,34}... | collective-permute-start | bytes 442376 | tf_op jit(solution)/shard_map/ppermute | solution.py:28
  250.1 10.2 %collective-permute-start.17 = (bf16[96,768]{1,0:T(8,128)(2,1)S(1)}, bf16[96,768]{1,0:T(8,128)(2,1)S(1)}, u32[]{:S(2)}, u32[]{:S(2)}) collective-permute-start(bf16[96,768]{1,0:T(8,128)(2,1)S(1)} %copy-done.7), channel_id=1, source_target_pairs={{0,16},{16,32},{32,48},{48,0},{1,17},{17,33},{33,49},{49,1},{2,18}... | collective-permute-start | bytes 442376 | tf_op jit(solution)/shard_map/ppermute | solution.py:28
  250.7 9.6 %collective-permute-start.18 = (bf16[96,768]{1,0:T(8,128)(2,1)S(1)}, bf16[96,768]{1,0:T(8,128)(2,1)S(1)}, u32[]{:S(2)}, u32[]{:S(2)}) collective-permute-start(bf16[96,768]{1,0:T(8,128)(2,1)S(1)} %copy-done.5), channel_id=1, source_target_pairs={{0,48},{16,0},{32,16},{48,32},{1,49},{17,1},{33,17},{49,33},{2,50}... | collective-permute-start | bytes 442376 | tf_op jit(solution)/shard_map/ppermute | solution.py:28
  255.4 12.6 %collective-permute-start.15 = (bf16[256,768]{1,0:T(8,128)(2,1)}, bf16[256,768]{1,0:T(8,128)(2,1)}, u32[]{:S(2)}, u32[]{:S(2)}) collective-permute-start(bf16[256,768]{1,0:T(8,128)(2,1)} %bitcast.27), channel_id=1, source_target_pairs={{0,64},{64,0},{1,65},{65,1},{2,66},{66,2},{3,67},{67,3},{4,68},{68... | collective-permute-start | bytes 1179656 | tf_op jit(solution)/shard_map/ppermute | solution.py:28
  260.4 6.8 %collective-permute-start.19 = (bf16[48,768]{1,0:T(8,128)(2,1)S(1)}, bf16[48,768]{1,0:T(8,128)(2,1)S(1)}, u32[]{:S(2)}, u32[]{:S(2)}) collective-permute-start(bf16[48,768]{1,0:T(8,128)(2,1)S(1)} %fusion.22), channel_id=1, source_target_pairs={{0,64},{64,0},{1,65},{65,1},{2,66},{66,2},{3,67},{67,3},{4,68},{68... | collective-permute-start | bytes 221192 | tf_op jit(solution)/shard_map/ppermute | solution.py:28
  262.4 3.5 %copy-start.14 = (f32[768,768]{1,0:T(8,128)S(1)}, f32[768,768]{1,0:T(8,128)}, u32[]{:S(2)}) copy-start(f32[768,768]{1,0:T(8,128)} %fusion.13) | copy-start | bytes 7077892
  265.9 2.1 copy-start.18
  265.9 4.6 %copy-start.1 = (bf16[768,768]{1,0:T(8,128)(2,1)S(1)}, bf16[768,768]{1,0:T(8,128)(2,1)}, u32[]{:S(2)}) copy-start(bf16[768,768]{1,0:T(8,128)(2,1)} %param.11) | copy-start | bytes 3538948
  (2 other events, 1.3 us)
Sparse Core Ops, SparseCore 0:
  10.3 44.7 all-gather.2
  64.9 37.8 reduce-scatter.2
  152.4 39.8 all-gather.4
  202.3 43.4 reduce-scatter.4

commit v2 on v1

--- a/solution.py
+++ b/solution.py
@@ -216,16 +216,14 @@
         return [lax.dynamic_index_in_dim(parts, at, 0, False) for at in (yh, 1 - yh)]
 
     both = lax.all_gather(jnp.stack(halves(tokens) + halves(cotangent)), ROW, axis=1, tiled=True)
-    w_in_turned, w_out_turned, bases = lax.optimization_barrier(
-        (w_in.T, w_out.T, basis_parts(left_basis, right_basis))
-    )
-
-    leaving = bf(matmul(both[3], w_out_turned))
+    w_in, w_out, bases = lax.optimization_barrier((w_in, w_out, basis_parts(left_basis, right_basis)))
+
+    leaving = bf(matmul(both[3], w_out, 1, 1))
     back_arrived = shift(leaving, "yh", 1)
     leaving, w_in_later = lax.optimization_barrier((leaving, w_in))
     terms = bf(matmul(both[:2].reshape(token_count, width), w_in_later)).reshape(2, half, width)
     forward = lax.psum_scatter(terms, "x", scatter_dimension=1, tiled=True)
-    staying = matmul(both[2], w_out_turned)
+    staying = matmul(both[2], w_out, 1, 1)
     line = both[:2].reshape(token_count, width).T
     back_arrived, staying, line = lax.optimization_barrier((back_arrived, staying, line))
 
@@ -252,7 +250,7 @@
     mixed_other = bf(matmul(act_other, w_out))
     grads, mixed_other = lax.optimization_barrier((grads, mixed_other))
 
-    carried = bf(matmul(grads.reshape(token_count, width), w_in_turned))
+    carried = bf(matmul(grads.reshape(token_count, width), w_in, 1, 1))
     terms = jnp.concatenate([mixed_own, mixed_other, carried]).reshape(8, half // 2, width)
     sums = lax.psum_scatter(terms, ("z", "c"), scatter_dimension=1, tiled=True)
     terms, grads = lax.optimization_barrier((terms, grads))

time: 278 us -> 278 us (level)
  no operation moved by 1% of the time
where the time goes in v2:
time: 278 us; the launch traced here: 277 us
  waiting for transfers between devices  134 us (48%)
  matrix products  41.9 us (15%)
  starting transfers between devices  32.3 us (12%)
  Pallas kernels  21.8 us (8%)
  local copies, waits for them, and re-layouts  17 us (6%)
  other arithmetic  15.9 us (6%)
  between operations  14 us (5%)
    ppermute x20, waiting for transfers between devices, shift(): lax.ppermute(value, axis, [(i, (i + by) % size) for i in range(size)])  94.1 us
    dot_general x11, matrix products, matmul(): lax.dot_general(a, b, (((ca,), (cb,)), ((), ())), preferred_element_type=...  41.9 us
    all_gather x1, waiting for transfers between devices, shards(): lax.all_gather(jnp.stack(halves(tokens) + halves(cotangent)), ROW, axis=1...  40 us
    ppermute x20, starting transfers between devices, shift(): lax.ppermute(value, axis, [(i, (i + by) % size) for i in range(size)])  32.1 us
    pallas_call x4, Pallas kernels, call(): pl.pallas_call(kernel, out_shape=out_shape, grid_spec=pltpu.PrefetchScala...  21.8 us
    unnamed x52, local copies, waits for them, and re-layouts  6.93 us
  transfers between devices with their start and end apart: 24, of which 11 were waited for; matrix products, arithmetic and copies ran while one was open for 16% of the time, Pallas kernels for 8%

profile of v2, /device:TPU:2, one launch (start us, length us, event | category | flops | bytes accessed | tf_op | source)
XLA Modules:
  0.0 277.0 jit_solution(9354456543551421033)
XLA Ops:
  7.2 1.2 constant_dynamic-slice_fusion.7
  9.3 4.8 %shard_map.143 = (bf16[768,768]{1,0:T(8,128)(2,1)S(1)}, bf16[768,768]{1,0:T(8,128)(2,1)S(1)}, bf16[768,768]{1,0:T(8,128)(2,1)S(1)}, bf16[768,768]{1,0:T(8,128)(2,1)}, bf16[768,768]{1,0:T(8,128)(2,1)}) custom-call(s32[1]{0:T(128)} %constant.90.clone.1._, f32[768,768]{1,0:T(8,128)} %left_ref.1, f32[768,768]{1,0:T(8,128)} %right_ref.1), custom_call_target="tpu_custom_call" | custom-call | bytes 10616832 | tf_op jit(solution)/shard_map/pallas_call | solution.py:58
  15.1 40.0 %all-gather.3.cloned.1.call-done = bf16[4,1024,768]{2,1,0:T(8,128)(2,1)} async-done(((bf16[4,64,768]{2,1,0:T(8,128)(2,1)}), bf16[4,1024,768]{2,1,0:T(8,128)(2,1)}) %all-gather.3.cloned.1.call-update) | async-done | bytes 6291472 | tf_op jit(solution)/shard_map/all_gather | solution.py:218
  55.1 4.1 %convolution_convert_fusion.4 = bf16[1024,768]{1,0:T(8,128)(2,1)} fusion(bf16[768,768]{1,0:T(8,128)(2,1)S(1)} %copy-done, bf16[4,1024,768]{2,1,0:T(8,128)(2,1)} %all-gather.3.cloned.1.call-done), kind=kOutput, calls=%fused_computation.8 | convolution fusion | flops 1208745984 | bytes 4325376 | tf_op jit(solution)/shard_map/dot_general | solution.py:39
  59.4 1.4 copy-done.25
  60.8 4.0 %convolution_convert_fusion.1 = bf16[2048,768]{1,0:T(8,128)(2,1)} fusion(bf16[2048,768]{1,0:T(8,128)(2,1)S(1)} %bitcast.79, bf16[768,768]{1,0:T(8,128)(2,1)S(1)} %copy-done.25), kind=kOutput, calls=%fused_computation.2 | convolution fusion | flops 2417491968 | bytes 7471104 | tf_op jit(solution)/shard_map/dot_general | solution.py:39
  64.9 2.9 %collective-permute-start = (bf16[1024,768]{1,0:T(8,128)(2,1)}, bf16[1024,768]{1,0:T(8,128)(2,1)}, u32[]{:S(2)}, u32[]{:S(2)}) collective-permute-start(bf16[1024,768]{1,0:T(8,128)(2,1)} %convolution_convert_fusion.4), channel_id=1, source_target_pairs={{0,1},{1,0},{2,3},{3,2},{4,5},{5,4},{6,7},{7,6},{8,9},{9,8},{10,11... | collective-permute-start | bytes 4718600 | tf_op jit(solution)/shard_map/ppermute | solution.py:28
  67.8 2.8 %fusion.14 = f32[1024,768]{1,0:T(8,128)S(1)} fusion(bf16[768,768]{1,0:T(8,128)(2,1)S(1)} %copy-done, bf16[4,1024,768]{2,1,0:T(8,128)(2,1)} %all-gather.3.cloned.1.call-done), kind=kOutput, calls=%fused_computation.22 | convolution fusion | flops 1207959552 | bytes 5898240 | tf_op jit(solution)/shard_map/dot_general | solution.py:39
  70.7 32.7 %collective-permute-done = bf16[1024,768]{1,0:T(8,128)(2,1)} collective-permute-done((bf16[1024,768]{1,0:T(8,128)(2,1)}, bf16[1024,768]{1,0:T(8,128)(2,1)}, u32[]{:S(2)}, u32[]{:S(2)}) %collective-permute-start) | collective-permute-done | bytes 1572896 | tf_op jit(solution)/shard_map/ppermute | solution.py:28
  103.3 1.9 add_convert_fusion
  105.2 1.2 constant_dynamic-slice_fusion.2
  107.5 2.9 %collective-permute-start.1 = (bf16[256,768]{1,0:T(8,128)(2,1)S(1)}, bf16[256,768]{1,0:T(8,128)(2,1)S(1)}, u32[]{:S(2)}, u32[]{:S(2)}) collective-permute-start(bf16[256,768]{1,0:T(8,128)(2,1)S(1)} %slice_bitcast_fusion.6), channel_id=1, source_target_pairs={{0,1},{1,0},{2,3},{3,2},{4,5},{5,4},{6,7},{7,6},{8,9},{9,8},{10,11... | collective-permute-start | bytes 1179656 | tf_op jit(solution)/shard_map/ppermute | solution.py:28
  110.4 2.1 collective-permute-start.2
  112.5 2.0 collective-permute-start.4
  114.5 5.0 %collective-permute-done.1 = bf16[256,768]{1,0:T(8,128)(2,1)S(1)} collective-permute-done((bf16[256,768]{1,0:T(8,128)(2,1)S(1)}, bf16[256,768]{1,0:T(8,128)(2,1)S(1)}, u32[]{:S(2)}, u32[]{:S(2)}) %collective-permute-start.1) | collective-permute-done | bytes 393248 | tf_op jit(solution)/shard_map/ppermute | solution.py:28
  119.5 1.4 fusion.19
  120.9 3.3 %collective-permute-done.2 = bf16[256,768]{1,0:T(8,128)(2,1)S(1)} collective-permute-done((bf16[256,768]{1,0:T(8,128)(2,1)}, bf16[256,768]{1,0:T(8,128)(2,1)S(1)}, u32[]{:S(2)}, u32[]{:S(2)}) %collective-permute-start.2) | collective-permute-done | bytes 393248 | tf_op jit(solution)/shard_map/ppermute | solution.py:28
  124.2 6.6 %collective-permute-done.3 = bf16[256,768]{1,0:T(8,128)(2,1)S(1)} collective-permute-done((bf16[256,768]{1,0:T(8,128)(2,1)}, bf16[256,768]{1,0:T(8,128)(2,1)S(1)}, u32[]{:S(2)}, u32[]{:S(2)}) %collective-permute-start.3) | collective-permute-done | bytes 393248 | tf_op jit(solution)/shard_map/ppermute | solution.py:28
  131.4 1.5 collective-permute-start.6
  132.8 3.2 %collective-permute-start.7 = (bf16[256,768]{1,0:T(8,128)(2,1)S(1)}, bf16[256,768]{1,0:T(8,128)(2,1)S(1)}, u32[]{:S(2)}, u32[]{:S(2)}) collective-permute-start(bf16[256,768]{1,0:T(8,128)(2,1)S(1)} %get-tuple-element.94), channel_id=1, source_target_pairs={{0,4},{2,6},{4,0},{6,2},{1,5},{3,7},{5,1},{7,3},{8,12},{10,14},{12... | collective-permute-start | bytes 1179656 | tf_op jit(solution)/shard_map/ppermute | solution.py:28
  137.0 1.2 broadcast_in_dim.3
  139.0 3.0 %collective-permute-done.5 = bf16[256,768]{1,0:T(8,128)(2,1)S(1)} collective-permute-done((bf16[256,768]{1,0:T(8,128)(2,1)S(1)}, bf16[256,768]{1,0:T(8,128)(2,1)S(1)}, u32[]{:S(2)}, u32[]{:S(2)}) %collective-permute-start.5) | collective-permute-done | bytes 393248 | tf_op jit(solution)/shard_map/ppermute | solution.py:28
  142.8 1.1 collective-permute-done.6
  144.7 5.8 %collective-permute-done.7 = bf16[256,768]{1,0:T(8,128)(2,1)S(1)} collective-permute-done((bf16[256,768]{1,0:T(8,128)(2,1)S(1)}, bf16[256,768]{1,0:T(8,128)(2,1)S(1)}, u32[]{:S(2)}, u32[]{:S(2)}) %collective-permute-start.7) | collective-permute-done | bytes 393248 | tf_op jit(solution)/shard_map/ppermute | solution.py:28
  153.2 4.0 %convolution_convert_fusion.3 = bf16[1024,768]{1,0:T(8,128)(2,1)} fusion(bf16[1024,768]{1,0:T(8,128)(2,1)} %constant_dynamic-update-slice_fusion, bf16[768,768]{1,0:T(8,128)(2,1)S(1)} %copy-done), kind=kOutput, calls=%fused_computation.7 | convolution fusion | flops 1208745984 | bytes 4325376 | tf_op jit(solution)/shard_map/dot_general | solution.py:39
  157.2 4.8 %fusion.13 = f32[768,768]{1,0:T(8,128)} fusion(bf16[1024,768]{1,0:T(8,128)(2,1)} %constant_dynamic-update-slice_fusion, bf16[4,1024,768]{2,1,0:T(8,128)(2,1)} %all-gather.3.cloned.1.call-done), kind=kOutput, calls=%fused_computation.21 | convolution fusion | flops 1207959552 | bytes 5505024 | tf_op jit(solution)/shard_map/dot_general | solution.py:39
  162.0 28.1 %collective-permute-done.9 = bf16[1024,768]{1,0:T(8,128)(2,1)S(1)} collective-permute-done((bf16[1024,768]{1,0:T(8,128)(2,1)}, bf16[1024,768]{1,0:T(8,128)(2,1)S(1)}, u32[]{:S(2)}, u32[]{:S(2)}) %collective-permute-start.9) | collective-permute-done | bytes 1572896 | tf_op jit(solution)/shard_map/ppermute | solution.py:28
  190.1 1.2 copy-done.24
  191.3 2.5 convolution_convert_fusion.2
  193.8 5.0 %convolution_convert_fusion = bf16[2048,768]{1,0:T(8,128)(2,1)S(1)} fusion(bf16[2048,768]{1,0:T(8,128)(2,1)} %bitcast.90, bf16[768,768]{1,0:T(8,128)(2,1)} %param.10), kind=kOutput, calls=%fused_computation.1 | convolution fusion | flops 2417491968 | bytes 7471104 | tf_op jit(solution)/shard_map/dot_general | solution.py:39
  198.9 3.3 %pad_maximum_fusion = bf16[4096,768]{1,0:T(8,128)(2,1)} fusion(bf16[2048,768]{1,0:T(8,128)(2,1)S(1)} %convolution_convert_fusion, bf16[1024,768]{1,0:T(8,128)(2,1)S(1)} %copy-done.16, bf16[1024,768]{1,0:T(8,128)(2,1)S(1)} %copy-done.15), kind=kLoop, calls=%fused_computation | loop fusion | flops 18874368 | bytes 12582912 | tf_op jit(solution)/shard_map/concatenate | solution.py:254
  202.3 3.5 %fusion = f32[768,768]{1,0:T(8,128)S(1)} fusion(bf16[2,1024,768]{2,1,0:T(8,128)(2,1)} %all-gather.5.cloned.1.call-done, bf16[768,2048]{0,1:T(8,128)(2,1)} %bitcast.80), kind=kOutput, calls=%fused_computation.11 | convolution fusion | flops 1207959552 | bytes 5505024 | tf_op jit(solution)/shard_map/dot_general | solution.py:39
  206.0 2.9 %add_multiply_fusion.weight_ref.w_ref = f32[768,768]{1,0:T(8,128)} fusion(f32[768,768]{1,0:T(8,128)S(1)} %fusion, bf16[2,1024,768]{2,1,0:T(8,128)(2,1)S(1)} %copy-done.23, bf16[768,2048]{0,1:T(8,128)(2,1)S(1)} %bitcast.81), kind=kOutput, calls=%fused_computation.5 | convolution fusion | flops 1209139200 | bytes 7864320 | tf_op jit(solution)/shard_map/dot_general | solution.py:39
  209.0 4.5 %shard_map.144 = (bf16[4,2,48,768]{3,2,1,0:T(8,128)(2,1)S(1)}, bf16[4,2,48,768]{3,2,1,0:T(8,128)(2,1)S(1)}, bf16[2,96,768]{2,1,0:T(8,128)(2,1)S(1)}, bf16[2,96,7...) custom-call(s32[4]{0:T(128)S(1)} %pad_add_fusion.1.at, ...), custom_call_target="tpu_custom_call" | custom-call | flops 1811939328 | bytes 4718592 | tf_op jit(solution)/shard_map/pallas_call | solution.py:58
  213.6 1.9 collective-permute-done.10
  215.5 4.5 %collective-permute-start.11 = (bf16[2,96,768]{2,1,0:T(8,128)(2,1)S(1)}, bf16[2,96,768]{2,1,0:T(8,128)(2,1)S(1)}, u32[]{:S(2)}, u32[]{:S(2)}) collective-permute-start(bf16[2,96,768]{2,1,0:T(8,128)(2,1)S(1)} %get-tuple-element.121), channel_id=1, source_target_pairs={{0,4},{2,6},{4,0},{6,2},{1,5},{3,7},{5,1},{7,3},{8,12},{10,14},{12... | collective-permute-start | bytes 884744 | tf_op jit(solution)/shard_map/ppermute | solution.py:28
  221.0 1.1 collective-permute-start.13
  224.1 11.9 %shard_map.146 = (f32[768,768]{1,0:T(8,128)}, f32[768,768]{1,0:T(8,128)}, bf16[768,768]{1,0:T(8,128)(2,1)S(1)}) custom-call(s32[1]{0:T(128)} %constant.90.clone.1._, f32[768,768]{1,0:T(8,128)} %add_multiply_fusion.weight_ref.w_ref, bf16[768,768]{1,0:T(8,128)(2,1)S(1)} %get-tuple-element.124.th_ref, bf16[768,768]{1,0:T(8,128)(2,1)S(1)} %copy-done.3, ...), custom_call_target="tpu_custom_call" | custom-call | flops 5435817984 | bytes 17694720 | tf_op jit(solution)/shard_map/pallas_call | solution.py:58
  238.8 6.6 %collective-permute-done.14 = bf16[96,768]{1,0:T(8,128)(2,1)S(1)} collective-permute-done((bf16[96,768]{1,0:T(8,128)(2,1)}, bf16[96,768]{1,0:T(8,128)(2,1)S(1)}, u32[]{:S(2)}, u32[]{:S(2)}) %collective-permute-start.14) | collective-permute-done | bytes 147488 | tf_op jit(solution)/shard_map/ppermute | solution.py:28
  245.4 1.9 bitcast_add_fusion
  247.2 2.9 %collective-permute-start.16 = (bf16[96,768]{1,0:T(8,128)(2,1)S(1)}, bf16[96,768]{1,0:T(8,128)(2,1)S(1)}, u32[]{:S(2)}, u32[]{:S(2)}) collective-permute-start(bf16[96,768]{1,0:T(8,128)(2,1)S(1)} %copy-done.9), channel_id=1, source_target_pairs={{0,32},{16,48},{32,0},{48,16},{1,33},{17,49},{33,1},{49,17},{2,34}... | collective-permute-start | bytes 442376 | tf_op jit(solution)/shard_map/ppermute | solution.py:28
  250.8 2.6 collective-permute-start.18
  253.3 2.0 constant_dynamic-slice_fusion.1
  255.6 4.8 %fusion.15 = f32[768,768]{1,0:T(8,128)} fusion(bf16[768,768]{1,0:T(8,128)(2,1)} %get-tuple-element.126.rh_ref, bf16[768,768]{1,0:T(8,128)(2,1)S(1)} %get-tuple-element.143, bf16[768,768]{1,0:T(8,128)(2,1)S(1)} %copy-done.11), kind=kOutput, calls=%fused_computation.24 | convolution fusion | flops 1812529152 | bytes 5898240 | tf_op jit(solution)/shard_map/dot_general | solution.py:39
  260.4 1.9 collective-permute-start.19
  262.4 3.5 %fusion.12 = f32[768,768]{1,0:T(8,128)S(1)} fusion(bf16[1024,768]{1,0:T(8,128)(2,1)} %copy-done.24, bf16[4,1024,768]{2,1,0:T(8,128)(2,1)} %all-gather.3.cloned.1.call-done), kind=kOutput, calls=%fused_computation.20 | convolution fusion | flops 1207959552 | bytes 5505024 | tf_op jit(solution)/shard_map/dot_general | solution.py:39
  265.9 1.4 multiply_convert_fusion
  268.0 1.1 fusion.20
  (99 shorter events, 19.0 us)
Async XLA Ops:
  7.2 47.9 %copy-start = (bf16[768,768]{1,0:T(8,128)(2,1)S(1)}, bf16[768,768]{1,0:T(8,128)(2,1)}, u32[]{:S(2)}) copy-start(bf16[768,768]{1,0:T(8,128)(2,1)} %param.11) | copy-start | bytes 3538948
  7.2 47.9 %all-gather.3.cloned.1.call-start = ((), (), s32[]{:S(2)}) async-start(), calls=%async_computation.2 | async-start | bytes 6684672 | tf_op jit(solution)/shard_map/all_gather | solution.py:218
  9.2 97.2 %reduce-scatter.3.cloned.1.call-start = ((), (), s32[]{:S(2)}) async-start(), calls=%async_computation.3 | async-start | bytes 3932160 | tf_op jit(solution)/shard_map/reduce_scatter | solution.py:225
  14.0 1.0 copy-start.2
  55.1 4.1 %copy-start.17 = (bf16[4,1024,768]{2,1,0:T(8,128)(2,1)S(1)}, bf16[4,1024,768]{2,1,0:T(8,128)(2,1)}, u32[]{:S(2)}) copy-start(bf16[4,1024,768]{2,1,0:T(8,128)(2,1)} %all-gather.3.cloned.1.call-done) | copy-start | bytes 18874372
  59.2 1.6 copy-start.25
  59.4 5.4 %copy-start.12 = (bf16[2,1024,768]{2,1,0:T(8,128)(2,1)}, bf16[2,1024,768]{2,1,0:T(8,128)(2,1)S(1)}, u32[]{:S(2)}) copy-start(bf16[2,1024,768]{2,1,0:T(8,128)(2,1)S(1)} %slice.95) | copy-start | bytes 9437188
  64.8 129.0 %all-gather.5.cloned.1.call-start = ((), (), s32[]{:S(2)}) async-start(), calls=%async_computation.4 | async-start | bytes 3932160 | tf_op jit(solution)/shard_map/all_gather | solution.py:245
  64.9 38.4 %collective-permute-start = (bf16[1024,768]{1,0:T(8,128)(2,1)}, bf16[1024,768]{1,0:T(8,128)(2,1)}, u32[]{:S(2)}, u32[]{:S(2)}) collective-permute-start(bf16[1024,768]{1,0:T(8,128)(2,1)} %convolution_convert_fusion.4), channel_id=1, source_target_pairs={{0,1},{1,0},{2,3},{3,2},{4,5},{5,4},{6,7},{7,6},{8,9},{9,8},{10,11... | collective-permute-start | bytes 4718600 | tf_op jit(solution)/shard_map/ppermute | solution.py:28
  106.4 29.7 %copy-start.19 = (bf16[256,768]{1,0:T(8,128)(2,1)S(1)}, bf16[256,768]{1,0:T(8,128)(2,1)}, u32[]{:S(2)}) copy-start(bf16[256,768]{1,0:T(8,128)(2,1)} %get-tuple-element.95) | copy-start | bytes 1179652
  107.5 12.0 %collective-permute-start.1 = (bf16[256,768]{1,0:T(8,128)(2,1)S(1)}, bf16[256,768]{1,0:T(8,128)(2,1)S(1)}, u32[]{:S(2)}, u32[]{:S(2)}) collective-permute-start(bf16[256,768]{1,0:T(8,128)(2,1)S(1)} %slice_bitcast_fusion.6), channel_id=1, source_target_pairs={{0,1},{1,0},{2,3},{3,2},{4,5},{5,4},{6,7},{7,6},{8,9},{9,8},{10,11... | collective-permute-start | bytes 1179656 | tf_op jit(solution)/shard_map/ppermute | solution.py:28
  110.4 13.8 %collective-permute-start.2 = (bf16[256,768]{1,0:T(8,128)(2,1)}, bf16[256,768]{1,0:T(8,128)(2,1)S(1)}, u32[]{:S(2)}, u32[]{:S(2)}) collective-permute-start(bf16[256,768]{1,0:T(8,128)(2,1)} %get-tuple-element.157), channel_id=1, source_target_pairs={{0,4},{2,6},{4,0},{6,2},{1,5},{3,7},{5,1},{7,3},{8,12},{10,14},{12... | collective-permute-start | bytes 1179656 | tf_op jit(solution)/shard_map/ppermute | solution.py:28
  112.5 18.3 %collective-permute-start.3 = (bf16[256,768]{1,0:T(8,128)(2,1)}, bf16[256,768]{1,0:T(8,128)(2,1)S(1)}, u32[]{:S(2)}, u32[]{:S(2)}) collective-permute-start(bf16[256,768]{1,0:T(8,128)(2,1)} %get-tuple-element.158), channel_id=1, source_target_pairs={{0,2},{2,4},{4,6},{6,0},{1,3},{3,5},{5,7},{7,1},{8,10},{10,12},{12... | collective-permute-start | bytes 1179656 | tf_op jit(solution)/shard_map/ppermute | solution.py:28
  112.5 18.3 %collective-permute-start.4 = (bf16[256,768]{1,0:T(8,128)(2,1)}, bf16[256,768]{1,0:T(8,128)(2,1)S(1)}, u32[]{:S(2)}, u32[]{:S(2)}) collective-permute-start(bf16[256,768]{1,0:T(8,128)(2,1)} %get-tuple-element.156), channel_id=1, source_target_pairs={{0,6},{2,0},{4,2},{6,4},{1,7},{3,1},{5,3},{7,5},{8,14},{10,8},{12,... | collective-permute-start | bytes 1179656 | tf_op jit(solution)/shard_map/ppermute | solution.py:28
  130.8 11.3 %collective-permute-start.5 = (bf16[256,768]{1,0:T(8,128)(2,1)S(1)}, bf16[256,768]{1,0:T(8,128)(2,1)S(1)}, u32[]{:S(2)}, u32[]{:S(2)}) collective-permute-start(bf16[256,768]{1,0:T(8,128)(2,1)S(1)} %get-tuple-element.94), channel_id=1, source_target_pairs={{0,6},{2,0},{4,2},{6,4},{1,7},{3,1},{5,3},{7,5},{8,14},{10,8},{12,... | collective-permute-start | bytes 1179656 | tf_op jit(solution)/shard_map/ppermute | solution.py:28
  131.4 12.6 %collective-permute-start.6 = (bf16[256,768]{1,0:T(8,128)(2,1)S(1)}, bf16[256,768]{1,0:T(8,128)(2,1)S(1)}, u32[]{:S(2)}, u32[]{:S(2)}) collective-permute-start(bf16[256,768]{1,0:T(8,128)(2,1)S(1)} %get-tuple-element.94), channel_id=1, source_target_pairs={{0,2},{2,4},{4,6},{6,0},{1,3},{3,5},{5,7},{7,1},{8,10},{10,12},{12... | collective-permute-start | bytes 1179656 | tf_op jit(solution)/shard_map/ppermute | solution.py:28
  132.8 17.7 %collective-permute-start.7 = (bf16[256,768]{1,0:T(8,128)(2,1)S(1)}, bf16[256,768]{1,0:T(8,128)(2,1)S(1)}, u32[]{:S(2)}, u32[]{:S(2)}) collective-permute-start(bf16[256,768]{1,0:T(8,128)(2,1)S(1)} %get-tuple-element.94), channel_id=1, source_target_pairs={{0,4},{2,6},{4,0},{6,2},{1,5},{3,7},{5,1},{7,3},{8,12},{10,14},{12... | collective-permute-start | bytes 1179656 | tf_op jit(solution)/shard_map/ppermute | solution.py:28
  136.3 15.0 %collective-permute-start.8 = (bf16[256,768]{1,0:T(8,128)(2,1)S(1)}, bf16[256,768]{1,0:T(8,128)(2,1)S(1)}, u32[]{:S(2)}, u32[]{:S(2)}) collective-permute-start(bf16[256,768]{1,0:T(8,128)(2,1)S(1)} %multiply_convert_fusion.1), channel_id=1, source_target_pairs={{0,1},{1,0},{2,3},{3,2},{4,5},{5,4},{6,7},{7,6},{8,9},{9,8},{10,11... | collective-permute-start | bytes 1179656 | tf_op jit(solution)/shard_map/ppermute | solution.py:28
  152.3 94.9 %reduce-scatter.5.cloned.1.call-start = ((), (), s32[]{:S(2)}) async-start(), calls=%async_computation.5 | async-start | bytes 7077888 | tf_op jit(solution)/shard_map/reduce_scatter | solution.py:255
  152.3 37.8 %collective-permute-start.9 = (bf16[1024,768]{1,0:T(8,128)(2,1)}, bf16[1024,768]{1,0:T(8,128)(2,1)S(1)}, u32[]{:S(2)}, u32[]{:S(2)}) collective-permute-start(bf16[1024,768]{1,0:T(8,128)(2,1)} %constant_dynamic-update-slice_fusion), channel_id=1, source_target_pairs={{0,1},{1,0},{2,3},{3,2},{4,5},{5,4},{6,7},{7,6},{8,9},{9,8},{10,11... | collective-permute-start | bytes 4718600 | tf_op jit(solution)/shard_map/ppermute | solution.py:28
  190.1 1.2 copy-start.24
  193.8 5.0 %copy-start.15 = (bf16[1024,768]{1,0:T(8,128)(2,1)S(1)}, bf16[1024,768]{1,0:T(8,128)(2,1)}, u32[]{:S(2)}) copy-start(bf16[1024,768]{1,0:T(8,128)(2,1)} %convolution_convert_fusion.3) | copy-start | bytes 4718596
  193.8 5.0 %copy-start.16 = (bf16[1024,768]{1,0:T(8,128)(2,1)S(1)}, bf16[1024,768]{1,0:T(8,128)(2,1)}, u32[]{:S(2)}) copy-start(bf16[1024,768]{1,0:T(8,128)(2,1)} %convolution_convert_fusion.2) | copy-start | bytes 4718596
  202.2 3.5 %copy-start.13 = (bf16[2,1024,768]{2,1,0:T(8,128)(2,1)S(1)}, bf16[2,1024,768]{2,1,0:T(8,128)(2,1)}, u32[]{:S(2)}) copy-start(bf16[2,1024,768]{2,1,0:T(8,128)(2,1)} %copy-done.12) | copy-start | bytes 9437188
  202.3 3.8 %copy-start.23 = (bf16[2,1024,768]{2,1,0:T(8,128)(2,1)S(1)}, bf16[2,1024,768]{2,1,0:T(8,128)(2,1)}, u32[]{:S(2)}) copy-start(bf16[2,1024,768]{2,1,0:T(8,128)(2,1)} %all-gather.5.cloned.1.call-done) | copy-start | bytes 9437188
  209.0 15.1 %copy-start.3 = (bf16[768,768]{1,0:T(8,128)(2,1)S(1)}, bf16[768,768]{1,0:T(8,128)(2,1)}, u32[]{:S(2)}) copy-start(bf16[768,768]{1,0:T(8,128)(2,1)} %copy-done.2) | copy-start | bytes 3538948
  213.5 2.1 collective-permute-start.10
  215.5 21.5 %collective-permute-start.11 = (bf16[2,96,768]{2,1,0:T(8,128)(2,1)S(1)}, bf16[2,96,768]{2,1,0:T(8,128)(2,1)S(1)}, u32[]{:S(2)}, u32[]{:S(2)}) collective-permute-start(bf16[2,96,768]{2,1,0:T(8,128)(2,1)S(1)} %get-tuple-element.121), channel_id=1, source_target_pairs={{0,4},{2,6},{4,0},{6,2},{1,5},{3,7},{5,1},{7,3},{8,12},{10,14},{12... | collective-permute-start | bytes 884744 | tf_op jit(solution)/shard_map/ppermute | solution.py:28
  220.1 17.0 %collective-permute-start.12 = (bf16[2,96,768]{2,1,0:T(8,128)(2,1)S(1)}, bf16[2,96,768]{2,1,0:T(8,128)(2,1)S(1)}, u32[]{:S(2)}, u32[]{:S(2)}) collective-permute-start(bf16[2,96,768]{2,1,0:T(8,128)(2,1)S(1)} %get-tuple-element.120), channel_id=1, source_target_pairs={{0,2},{2,4},{4,6},{6,0},{1,3},{3,5},{5,7},{7,1},{8,10},{10,12},{12... | collective-permute-start | bytes 884744 | tf_op jit(solution)/shard_map/ppermute | solution.py:28
  221.0 16.1 %collective-permute-start.13 = (bf16[2,96,768]{2,1,0:T(8,128)(2,1)S(1)}, bf16[2,96,768]{2,1,0:T(8,128)(2,1)S(1)}, u32[]{:S(2)}, u32[]{:S(2)}) collective-permute-start(bf16[2,96,768]{2,1,0:T(8,128)(2,1)S(1)} %get-tuple-element.122), channel_id=1, source_target_pairs={{0,6},{2,0},{4,2},{6,4},{1,7},{3,1},{5,3},{7,5},{8,14},{10,8},{12,... | collective-permute-start | bytes 884744 | tf_op jit(solution)/shard_map/ppermute | solution.py:28
  224.1 11.9 %copy-start.4 = (bf16[96,768]{1,0:T(8,128)(2,1)}, bf16[96,768]{1,0:T(8,128)(2,1)S(1)}, u32[]{:S(2)}) copy-start(bf16[96,768]{1,0:T(8,128)(2,1)S(1)} %get-tuple-element.142) | copy-start | bytes 442372
  236.0 1.0 copy-start.10
  237.0 10.2 %copy-start.9 = (bf16[96,768]{1,0:T(8,128)(2,1)S(1)}, bf16[96,768]{1,0:T(8,128)(2,1)}, u32[]{:S(2)}) copy-start(bf16[96,768]{1,0:T(8,128)(2,1)} %copy-done.8) | copy-start | bytes 442372
  237.0 13.1 %copy-start.7 = (bf16[96,768]{1,0:T(8,128)(2,1)S(1)}, bf16[96,768]{1,0:T(8,128)(2,1)}, u32[]{:S(2)}) copy-start(bf16[96,768]{1,0:T(8,128)(2,1)} %copy-done.6) | copy-start | bytes 442372
  237.0 0.7 copy-start.20
  237.0 13.7 %copy-start.5 = (bf16[96,768]{1,0:T(8,128)(2,1)S(1)}, bf16[96,768]{1,0:T(8,128)(2,1)}, u32[]{:S(2)}) copy-start(bf16[96,768]{1,0:T(8,128)(2,1)} %copy-done.4) | copy-start | bytes 442372
  237.1 1.4 copy-start.21
  237.1 1.4 copy-start.22
  237.7 17.8 %copy-start.11 = (bf16[768,768]{1,0:T(8,128)(2,1)S(1)}, bf16[768,768]{1,0:T(8,128)(2,1)}, u32[]{:S(2)}) copy-start(bf16[768,768]{1,0:T(8,128)(2,1)} %copy-done.10) | copy-start | bytes 3538948
  238.5 6.9 %collective-permute-start.14 = (bf16[96,768]{1,0:T(8,128)(2,1)}, bf16[96,768]{1,0:T(8,128)(2,1)S(1)}, u32[]{:S(2)}, u32[]{:S(2)}) collective-permute-start(bf16[96,768]{1,0:T(8,128)(2,1)} %fusion.21), channel_id=1, source_target_pairs={{0,1},{1,0},{2,3},{3,2},{4,5},{5,4},{6,7},{7,6},{8,9},{9,8},{10,11... | collective-permute-start | bytes 442376 | tf_op jit(solution)/shard_map/ppermute | solution.py:28
  247.2 13.1 %collective-permute-start.16 = (bf16[96,768]{1,0:T(8,128)(2,1)S(1)}, bf16[96,768]{1,0:T(8,128)(2,1)S(1)}, u32[]{:S(2)}, u32[]{:S(2)}) collective-permute-start(bf16[96,768]{1,0:T(8,128)(2,1)S(1)} %copy-done.9), channel_id=1, source_target_pairs={{0,32},{16,48},{32,0},{48,16},{1,33},{17,49},{33,1},{49,17},{2,34}... | collective-permute-start | bytes 442376 | tf_op jit(solution)/shard_map/ppermute | solution.py:28
  250.1 10.2 %collective-permute-start.17 = (bf16[96,768]{1,0:T(8,128)(2,1)S(1)}, bf16[96,768]{1,0:T(8,128)(2,1)S(1)}, u32[]{:S(2)}, u32[]{:S(2)}) collective-permute-start(bf16[96,768]{1,0:T(8,128)(2,1)S(1)} %copy-done.7), channel_id=1, source_target_pairs={{0,16},{16,32},{32,48},{48,0},{1,17},{17,33},{33,49},{49,1},{2,18}... | collective-permute-start | bytes 442376 | tf_op jit(solution)/shard_map/ppermute | solution.py:28
  250.8 9.6 %collective-permute-start.18 = (bf16[96,768]{1,0:T(8,128)(2,1)S(1)}, bf16[96,768]{1,0:T(8,128)(2,1)S(1)}, u32[]{:S(2)}, u32[]{:S(2)}) collective-permute-start(bf16[96,768]{1,0:T(8,128)(2,1)S(1)} %copy-done.5), channel_id=1, source_target_pairs={{0,48},{16,0},{32,16},{48,32},{1,49},{17,1},{33,17},{49,33},{2,50}... | collective-permute-start | bytes 442376 | tf_op jit(solution)/shard_map/ppermute | solution.py:28
  255.4 12.6 %collective-permute-start.15 = (bf16[256,768]{1,0:T(8,128)(2,1)}, bf16[256,768]{1,0:T(8,128)(2,1)}, u32[]{:S(2)}, u32[]{:S(2)}) collective-permute-start(bf16[256,768]{1,0:T(8,128)(2,1)} %bitcast.25), channel_id=1, source_target_pairs={{0,64},{64,0},{1,65},{65,1},{2,66},{66,2},{3,67},{67,3},{4,68},{68... | collective-permute-start | bytes 1179656 | tf_op jit(solution)/shard_map/ppermute | solution.py:28
  260.4 6.8 %collective-permute-start.19 = (bf16[48,768]{1,0:T(8,128)(2,1)S(1)}, bf16[48,768]{1,0:T(8,128)(2,1)S(1)}, u32[]{:S(2)}, u32[]{:S(2)}) collective-permute-start(bf16[48,768]{1,0:T(8,128)(2,1)S(1)} %fusion.22), channel_id=1, source_target_pairs={{0,64},{64,0},{1,65},{65,1},{2,66},{66,2},{3,67},{67,3},{4,68},{68... | collective-permute-start | bytes 221192 | tf_op jit(solution)/shard_map/ppermute | solution.py:28
  262.4 3.5 %copy-start.14 = (f32[768,768]{1,0:T(8,128)S(1)}, f32[768,768]{1,0:T(8,128)}, u32[]{:S(2)}) copy-start(f32[768,768]{1,0:T(8,128)} %fusion.13) | copy-start | bytes 7077892
  265.9 2.1 copy-start.18
  265.9 4.6 %copy-start.1 = (bf16[768,768]{1,0:T(8,128)(2,1)S(1)}, bf16[768,768]{1,0:T(8,128)(2,1)}, u32[]{:S(2)}) copy-start(bf16[768,768]{1,0:T(8,128)(2,1)} %param.11) | copy-start | bytes 3538948
  (2 other events, 1.3 us)
Sparse Core Ops, SparseCore 0:
  10.3 44.7 all-gather.2
  64.9 37.8 reduce-scatter.2
  152.4 39.8 all-gather.4
  202.3 43.4 reduce-scatter.4
